TPU v7x, 256 devices: a whole 4x4x8 slice. The times are simulated.
256 devices in a mesh: grp: 8 (over y, core), seq: 32 (over z, x).
Axes of the slice: x: 4, y: 4, z: 8, core: 2. Of those that a mesh axis runs over, the one named last changes fastest.
Arguments:
- queries: bfloat16 [32768, 8192], P(('grp', 'seq')), may hold values from -120 to 120
- key_rows: bfloat16 [32768, 512], P(('grp', 'seq')), may hold values from -6 to 6
- value_rows: bfloat16 [32768, 512], P(('grp', 'seq')), may hold values from -6 to 6
- grad_rows: bfloat16 [32768, 8192], P(('grp', 'seq')), may hold values from -6 to 6
- targets: int32 [32768], P(('grp', 'seq')), may hold values from 0 to 32767, as said below
- doc_lengths: int32 [8, 16], P('grp'), may hold values from 1 to 512, 4096 in all within a row
Outputs:
- grad_query: bfloat16 [32768, 8192], P(('grp', 'seq'))
- grad_key: bfloat16 [32768, 512], P(('grp', 'seq'))
- grad_value: bfloat16 [32768, 512], P(('grp', 'seq'))
Inputs may be any that keep to these rules, and one draw needn't show every extreme that they name: targets is a permutation of the 32768 grouped rows; the grouped row of a loader row lies on the device with the same seq index in the group given by the row; at most 24 rows of one device go to one device, and every device receives exactly 24 rows from some device.
All inputs are finite; a program needn't handle non-finite values.
Results may differ from a plain program's by a relative error of at most 0.0095.
Values may be sent and summed in bfloat16 or wider, within the bound.
No kernel may reach another device: no remote copies, remote signals or barrier semaphores. Data moves between devices by JAX's collectives and lax.ppermute only.
A program may use at most 64 MiB of HBM per device.

v0:
```python
import functools

import jax
import jax.numpy as jnp
from jax import lax
from jax.experimental import pallas as pl
from jax.experimental.pallas import tpu as pltpu
from jax.sharding import PartitionSpec as P

HD = 128
KVH = 4
GQ = 16
DOCS = 16
ROWS = 128
CAP = 24
BACK = 4
WIN = (BACK + 1) * ROWS
EARLY = 2
CALLS = ((0, EARLY, 0), (EARLY, KVH - EARLY, 1))
SUMS = ((0, EARLY), (EARLY, KVH - EARLY))
WIDE = GQ * HD
SCALE = HD**-0.5
LOG2E = 1.4426950408889634
GROUPS = 8
FAR = 4
NEAR = (2, 3, 6, 7)
MSG = 2 * CAP
BSLOT = 64
PAIR = 256
A_PAIRS = GQ * ROWS // PAIR
B_PAIRS = GQ * BSLOT // PAIR
UNROLL = 4
f32, bf16, i32 = jnp.float32, jnp.bfloat16, jnp.int32
NT = (((1,), (1,)), ((), ()))


def dot(a, b, dims=None):
    if dims is None:
        return jnp.dot(a, b, preferred_element_type=f32)
    return lax.dot_general(a, b, dims, preferred_element_type=f32)


def iota(shape, dim):
    return lax.broadcasted_iota(i32, shape, dim)


def params(mib):
    return pltpu.CompilerParams(vmem_limit_bytes=mib * 1024 * 1024)


def arrival(group, hot, before, axis):
    if axis == 0:
        earlier = dot(hot.astype(bf16), before.astype(bf16))
    else:
        earlier = dot(before.astype(bf16), hot.astype(bf16))
    return jnp.sum(hot * earlier, axis=axis, keepdims=True).astype(i32)


def pack_keys(me_ref, length_ref, row_ref, col_ref, key_ref, value_ref, out_ref, order_ref, sort_ref):
    me = me_ref[0]
    group = row_ref[...] >> 12
    hot = (iota((GROUPS, ROWS), 0) == group).astype(f32)
    rank = arrival(group, hot, iota((ROWS, ROWS), 0) < iota((ROWS, ROWS), 1), 0)
    n = iota((GROUPS * MSG, ROWS), 0)
    both = (n == group * MSG + rank) | (n == (group ^ FAR) * MSG + CAP + rank)
    target = col_ref[...]
    group = target >> 12
    hot = (iota((ROWS, ROWS), 1) == group).astype(f32)
    rank = arrival(group, hot, iota((ROWS, ROWS), 1) < iota((ROWS, ROWS), 0), 1)
    order_ref[...] = (iota((ROWS, PAIR), 1) == (group ^ me) * CAP + rank).astype(bf16)
    n = iota((ROWS, GROUPS * MSG), 1)
    sort_ref[...] = ((n == group * MSG + rank) | (n == (group ^ FAR) * MSG + CAP + rank)).astype(bf16)
    lane = iota((1, HD), 1)
    slot = jnp.where(iota((ROWS, HD), 1) == 0, (target & (ROWS - 1)) + 1, 0).astype(f32).astype(bf16)
    extra = jnp.zeros((1, HD), i32)
    for k in range(DOCS):
        extra = jnp.where(lane == DOCS + k, length_ref[k] >> 8, extra)
        extra = jnp.where(lane == 2 * DOCS + k, length_ref[k] & 255, extra)
    parts = []
    for j in range(KVH):
        parts += [key_ref[:, j * HD : (j + 1) * HD], value_ref[:, j * HD : (j + 1) * HD]]
    packed = dot(both.astype(bf16), jnp.concatenate(parts + [slot], axis=1))
    out_ref[:, : KVH * 2 * HD] = packed[:, : KVH * 2 * HD].astype(bf16)
    out_ref[:, KVH * 2 * HD :] = (packed[:, KVH * 2 * HD :] + extra.astype(f32)).astype(bf16)


def pack_rows(blocks, me_ref, target_ref, mate_target_ref, query_ref, grad_ref, mate_query_ref, mate_grad_ref, _, *refs):
    outs, picks_ref = refs[:-1], refs[-1]
    @pl.when(pl.program_id(0) == 0)
    def _():
        for loader, ref in enumerate((target_ref, mate_target_ref)):
            group = ref[...] >> 12
            hot = (iota((GROUPS, ROWS), 0) == group).astype(f32)
            rank = arrival(group, hot, iota((ROWS, ROWS), 0) < iota((ROWS, ROWS), 1), 0)
            offset = group ^ me_ref[0]
            place = jnp.where((offset & 1) == 0, (offset >> 1) * MSG + loader * CAP + rank, -1)
            picks_ref[loader] = (iota((GROUPS * CAP, ROWS), 0) == place).astype(bf16)

    picks = [
        jnp.concatenate([picks_ref[loader, i * MSG : (i + 1) * MSG, :] for i in blocks], axis=0)
        for loader in range(2)
    ]
    query = dot(picks[0], query_ref[...]) + dot(picks[1], mate_query_ref[...])
    grad = dot(picks[0], grad_ref[...]) + dot(picks[1], mate_grad_ref[...])
    for i, ref in enumerate(outs):
        at = slice(i * MSG, (i + 1) * MSG)
        ref[...] = jnp.concatenate([query[at], grad[at]], axis=0).astype(bf16)


def starts_of(lengths, position):
    before = (iota((HD, HD), 0) <= iota((HD, HD), 1)).astype(bf16)
    high, low = lengths
    ends = 256.0 * dot(high.astype(bf16), before) + dot(low.astype(bf16), before)
    ends = jnp.broadcast_to(ends[0:1], (ROWS, HD))
    held = (ends <= position.astype(f32)) & (iota((ROWS, HD), 1) < DOCS)
    return jnp.max(jnp.where(held, ends, 0.0), axis=1, keepdims=True)


def group_keys(me_ref, seq_ref, msg_ref, whole_ref, early_ref, late_ref, spread_ref, dense_ref, back_ref, vec_ref):
    wide = KVH * 2 * HD
    me = me_ref[0]
    first = (seq_ref[0] - BACK) * ROWS
    slot = msg_ref[:, wide : wide + 1].astype(f32)
    n, r = iota((GROUPS * MSG, ROWS), 0), iota((GROUPS * MSG, ROWS), 1)
    side_of = jnp.zeros_like(n)
    for k in range(GROUPS):
        side_of = jnp.where((n >= k * MSG + CAP) & (n < (k + 1) * MSG), 1, side_of)
    whole = []
    for side in range(2):
        hot = ((slot == (r + 1).astype(f32)) & (side_of == side)).astype(f32)
        spread_ref[side * GROUPS * MSG : (side + 1) * GROUPS * MSG, :] = hot.astype(bf16)
        whole.append(dot(jnp.transpose(hot).astype(bf16), msg_ref[:, :wide]).astype(bf16))
    whole_ref[...] = jnp.concatenate(whole, axis=0)
    for ref, at in ((early_ref, slice(0, EARLY * 2 * HD)), (late_ref, slice(EARLY * 2 * HD, wide))):
        ref[...] = jnp.concatenate([w[:, at] for w in whole], axis=0)

    def message(k):
        at = pl.multiple_of((me ^ k) * MSG, MSG)
        return msg_ref[pl.ds(at, MSG), wide : wide + HD].astype(f32)

    from_own, from_core = message(0), message(1)
    a_slots = [m[:CAP, :1] for m in [from_own, from_core] + [message(k) for k in NEAR]]
    twice = []
    for i in range(0, 6, 2):
        twice += a_slots[i : i + 2] * 2
    rows = 12 * CAP
    column = jnp.concatenate(twice + [jnp.zeros((384 - rows, 1), f32)], axis=0)
    lane = iota((384, 2 * ROWS), 1)
    n = iota((384, 2 * ROWS), 0)
    is_grad = jnp.zeros_like(n)
    for k in range(3):
        is_grad = jnp.where((n >= (2 * k + 1) * MSG) & (n < (2 * k + 2) * MSG), 1, is_grad)
    hot = (column == ((lane & (ROWS - 1)) + 1).astype(f32)) & (is_grad == (lane >> 7))
    dense_ref[...] = jnp.transpose(hot.astype(f32)).astype(bf16)
    column = jnp.concatenate(a_slots, axis=0)
    back_ref[...] = (column == (iota((6 * CAP, ROWS), 1) + 1).astype(f32)).astype(bf16)

    def lengths(rows):
        rows = jnp.broadcast_to(rows[:1], (8, HD))
        pick = (iota((HD, HD), 0) == iota((HD, HD), 1) + DOCS).astype(bf16)
        high = dot(rows.astype(bf16), pick)
        pick = (iota((HD, HD), 0) == iota((HD, HD), 1) + 2 * DOCS).astype(bf16)
        return high, dot(rows.astype(bf16), pick)

    row, column = iota((ROWS, ROWS), 0), iota((ROWS, ROWS), 1)
    position = iota((ROWS, 1), 0) + first + BACK * ROWS
    gap = jnp.zeros((BSLOT - 2 * CAP, 1), f32)
    half = [from_own[CAP:, :1], from_core[CAP:, :1], gap]
    arrived = jnp.concatenate(half + half, axis=0)
    hot_b = jnp.transpose((arrived == (column + 1).astype(f32)).astype(f32))
    hots = ((row == column).astype(f32), hot_b)
    for side in range(2):
        start = starts_of(lengths(from_own if side == 0 else message(FAR)), position) - first.astype(f32)
        low = jnp.sum(hots[side] * start, axis=0, keepdims=True)
        high = jnp.sum(hots[side] * (row + BACK * ROWS).astype(f32), axis=0, keepdims=True)
        vec_ref[2 * side : 2 * side + 1, :] = low.astype(i32)
        vec_ref[2 * side + 1 : 2 * side + 2, :] = high.astype(i32)
    vec_ref[4:8, :] = jnp.zeros((4, ROWS), i32)


def attend(x_ref, dense_ref, back_ref, vec_ref, *refs):
    ins, refs = refs[:4], refs[4:]
    window, refs = refs[: BACK + 1], refs[BACK + 1 :]
    refs = refs[len(refs) - 9 - 8 :]
    outs, refs = refs[:6], refs[6:]
    (sums_ref, far_ref), refs = refs[:2], refs[2:]
    bias_ref, q_ref, g_ref, dq_ref, key_ref, value_ref, flip_ref, dk_ref, dv_ref = refs

    @pl.when(pl.program_id(0) == 0)
    def _():
        c = iota((WIN, ROWS), 0)
        for side in range(2):
            low, high = vec_ref[2 * side : 2 * side + 1, :], vec_ref[2 * side + 1 : 2 * side + 2, :]
            bias = jnp.where((c >= low) & (c <= high), 0.0, -1e30).astype(f32)
            bias_ref[side, :, 0:ROWS] = bias
            bias_ref[side, :, ROWS : 2 * ROWS] = bias

    pieces = [r[...] for r in ins[:3]]
    pieces.append(jnp.zeros((384 - 12 * CAP, WIDE), bf16))
    rows_a = dot(dense_ref[...], jnp.concatenate(pieces, axis=0)).astype(bf16)
    gap = jnp.zeros((BSLOT - MSG, WIDE), bf16)
    rows_b = jnp.concatenate([ins[3][:MSG], gap, ins[3][MSG:], gap], axis=0)
    for h in range(GQ):
        at = slice(h * HD, (h + 1) * HD)
        q_ref[h * ROWS : (h + 1) * ROWS, :] = rows_a[:ROWS, at]
        g_ref[h * ROWS : (h + 1) * ROWS, :] = rows_a[ROWS:, at]
        to = GQ * ROWS + h * BSLOT
        q_ref[to : to + BSLOT, :] = rows_b[:BSLOT, at]
        g_ref[to : to + BSLOT, :] = rows_b[BSLOT:, at]

    for side in range(2):
        for k in range(BACK + 1):
            part = window[k][side * ROWS : (side + 1) * ROWS, :]
            key_ref[k * ROWS : (k + 1) * ROWS, :] = part[:, :HD]
            value_ref[k * ROWS : (k + 1) * ROWS, :] = part[:, HD:]
            flip_ref[:, k * ROWS : (k + 1) * ROWS] = jnp.transpose(part[:, :HD].astype(f32)).astype(bf16)
        dk_ref[...] = jnp.zeros_like(dk_ref)
        dv_ref[...] = jnp.zeros_like(dv_ref)

        def pair(at):
            q, g = q_ref[pl.ds(at, PAIR), :], g_ref[pl.ds(at, PAIR), :]
            scores = dot(key_ref[...], q, NT) * (SCALE * LOG2E) + bias_ref[side]
            powers = jnp.exp2(scores - jnp.max(scores, axis=0, keepdims=True))
            probs = powers * (1.0 / jnp.sum(powers, axis=0, keepdims=True))
            dprobs = dot(value_ref[...], g, NT)
            weighted = probs * dprobs
            delta = jnp.sum(weighted, axis=0, keepdims=True)
            return probs.astype(bf16), (weighted - probs * delta).astype(bf16)

        @pl.loop(0, (B_PAIRS if side else A_PAIRS) // UNROLL)
        def _(step):
            wide = UNROLL * PAIR
            at = pl.multiple_of(step * wide + (A_PAIRS * PAIR if side else 0), PAIR)
            parts = [pair(at + u * PAIR) for u in range(UNROLL)]
            probs = jnp.concatenate([p for p, _ in parts], axis=1)
            dscores = jnp.concatenate([d for _, d in parts], axis=1)
            dv_ref[...] += dot(probs, g_ref[pl.ds(at, wide), :])
            dk_ref[...] += dot(dscores, q_ref[pl.ds(at, wide), :])
            dq_ref[:, pl.ds(at, wide)] = (dot(flip_ref[...], dscores) * SCALE).astype(bf16)

        for k in range(BACK + 1):
            at = slice(k * ROWS, (k + 1) * ROWS)
            both = jnp.concatenate([dk_ref[at, :] * SCALE, dv_ref[at, :]], axis=1).astype(bf16)
            if k == 0:
                far_ref[side * ROWS : (side + 1) * ROWS, :] = both
            else:
                to = ((x_ref[0] + k) & 3) * (2 * ROWS) + side * ROWS
                sums_ref[pl.ds(pl.multiple_of(to, ROWS), ROWS), :] = both

    back = back_ref[...]
    eye = (iota((ROWS, ROWS), 0) == iota((ROWS, ROWS), 1)).astype(bf16)
    straight = []
    for i in range(GQ // 2):
        from_ = GQ * ROWS + i * ROWS
        straight.append(dot(eye, dq_ref[:, from_ : from_ + ROWS], NT))
    for h in range(GQ):
        at = slice(h * HD, (h + 1) * HD)
        rows = dot(back, dq_ref[:, h * ROWS : (h + 1) * ROWS], NT)
        low = h % 2 * BSLOT
        extra = straight[h // 2][low : low + 2 * CAP]
        outs[0][:, at] = jnp.concatenate([rows[:CAP], extra[:CAP]], axis=0).astype(bf16)
        outs[1][:, at] = jnp.concatenate([rows[CAP : 2 * CAP], extra[CAP:]], axis=0).astype(bf16)
        if h < GQ // 2:
            early = rows if h == 0 else jnp.concatenate([early, rows], axis=1)
        else:
            late = rows if h == GQ // 2 else jnp.concatenate([late, rows], axis=1)
    for k in range(4):
        at = slice((k + 2) * CAP, (k + 3) * CAP)
        outs[k + 2][...] = jnp.concatenate([early[at], late[at]], axis=0).astype(bf16)


def add_blocks(x_ref, ref, later):
    total = jnp.zeros((2 * ROWS, ref.shape[1]), f32)
    for j in range(4):
        weight = jnp.where((j >= x_ref[0]) == later, 1.0, 0.0).astype(f32)
        total = total + ref[j * 2 * ROWS : (j + 1) * 2 * ROWS, :].astype(f32) * weight
    return total


def pass_on(x_ref, sums_ref, far_ref, out_ref):
    out_ref[...] = (add_blocks(x_ref, sums_ref, False) + far_ref[...].astype(f32)).astype(bf16)


def return_keys(x_ref, spread_ref, *refs):
    ins, out_ref = refs[:-1], refs[-1]
    size = GROUPS * MSG
    for part, (first, count) in enumerate(SUMS):
        total = add_blocks(x_ref, ins[2 * part], True) + ins[2 * part + 1][...].astype(f32)
        total = total.astype(bf16)
        rows = dot(spread_ref[:size, :], total[:ROWS]) + dot(spread_ref[size:, :], total[ROWS:])
        out_ref[:, first * 2 * HD : (first + count) * 2 * HD] = rows.astype(bf16)


def unpack_keys(sort_ref, msg_ref, key_ref, value_ref):
    rows = dot(sort_ref[...], msg_ref[...]).astype(bf16)
    for j in range(KVH):
        key_ref[:, j * HD : (j + 1) * HD] = rows[:, 2 * j * HD : (2 * j + 1) * HD]
        value_ref[:, j * HD : (j + 1) * HD] = rows[:, (2 * j + 1) * HD : (2 * j + 2) * HD]


def unpack_rows(order_ref, own_ref, core_ref, *refs):
    near, out_ref = refs[:4], refs[-1]
    own, core = own_ref[...].astype(f32), core_ref[...].astype(f32)
    near = [r[...].astype(f32) for r in near]
    near = [jnp.concatenate([r[:CAP], r[CAP:]], axis=1) for r in near]
    rows = [own[:CAP], core[:CAP], near[0], near[1], own[CAP:], core[CAP:], near[2], near[3]]
    rows.append(jnp.zeros((PAIR - 8 * CAP, WIDE), f32))
    out_ref[...] = dot(order_ref[...], jnp.concatenate(rows, axis=0).astype(bf16)).astype(bf16)


def shape(*dims, dtype=bf16):
    return jax.ShapeDtypeStruct(dims, dtype)


def full(*dims):
    return pl.BlockSpec(dims, lambda *_: (0,) * len(dims))


def columns(rows, wide, first=0):
    return pl.BlockSpec((rows, wide), lambda i: (0, first + i))


SMEM = pl.BlockSpec(memory_space=pltpu.SMEM)


def cost(flops, size, powers=0):
    return pl.CostEstimate(flops=int(flops), bytes_accessed=int(size), transcendentals=int(powers))


def on_device(queries, key_rows, value_rows, grad_rows, targets, doc_lengths):
    seq_count = lax.axis_size("seq")
    me = lax.axis_index("grp").astype(i32).reshape(1)
    seq = lax.axis_index("seq").astype(i32).reshape(1)

    def swap(tensor, k):
        return lax.ppermute(tensor, "grp", [(i, i ^ k) for i in range(GROUPS)])

    def later(tensor, distance):
        return lax.ppermute(tensor, "seq", [(i, (i + distance) % seq_count) for i in range(seq_count)])

    def earlier(tensor, distance):
        return lax.ppermute(tensor, "seq", [((i + distance) % seq_count, i) for i in range(seq_count)])

    wide = KVH * 2 * HD
    message, order, sort = pl.pallas_call(
        pack_keys,
        out_shape=[
            shape(GROUPS * MSG, wide + HD),
            shape(ROWS, PAIR),
            shape(ROWS, GROUPS * MSG),
        ],
        in_specs=[SMEM] * 2 + [pl.BlockSpec(memory_space=pltpu.VMEM)] * 4,
        compiler_params=params(32),
        cost_estimate=cost(1e8, 1 << 20),
        name="pack_keys",
    )(me, doc_lengths[0], targets.reshape(1, ROWS), targets.reshape(ROWS, 1), key_rows, value_rows)
    message = lax.all_to_all(message, "grp", split_axis=0, concat_axis=0, tiled=True)

    step = 1024
    mate_target = swap(targets, 1)
    mate_query, mate_grad = swap(queries, 1), swap(grad_rows, 1)
    def pack(blocks, first, count, after):
        return pl.pallas_call(
            functools.partial(pack_rows, blocks),
            grid=(count * WIDE // step,),
            out_shape=[shape(2 * MSG, count * WIDE)] * len(blocks),
            in_specs=[SMEM]
            + [full(1, ROWS)] * 2
            + [columns(ROWS, step, first * (WIDE // step))] * 4
            + [pl.BlockSpec(memory_space=pl.ANY)],
            out_specs=[columns(2 * MSG, step)] * len(blocks),
            scratch_shapes=[pltpu.VMEM((2, GROUPS * CAP, ROWS), bf16)],
            compiler_params=params(60),
            cost_estimate=cost(count * 1e8, count * 2 << 20),
            name="pack_rows",
        )(me, targets.reshape(1, ROWS), mate_target.reshape(1, ROWS), queries, grad_rows, mate_query, mate_grad, after)

    early = pack((1, 3), 0, EARLY, order)
    late = pack((1, 3), EARLY, KVH - EARLY, order)
    *rows, message = lax.optimization_barrier((*early, *late, message))
    early, late = rows[:2], rows[2:]
    early = [swap(early[0], 2), swap(early[1], 6)]

    whole, *own, spread, dense, back, vec = pl.pallas_call(
        group_keys,
        out_shape=[
            shape(2 * ROWS, wide),
            shape(2 * ROWS, EARLY * 2 * HD),
            shape(2 * ROWS, wide - EARLY * 2 * HD),
            shape(2 * GROUPS * MSG, ROWS),
            shape(2 * ROWS, 384),
            shape(6 * CAP, ROWS),
            shape(8, ROWS, dtype=i32),
        ],
        in_specs=[SMEM] * 2 + [pl.BlockSpec(memory_space=pltpu.VMEM)],
        compiler_params=params(32),
        cost_estimate=cost(2e8, 2 << 20),
        name="group_keys",
    )(me, seq, message)

    x = seq & 3
    whole = later(whole, 3)
    windows = []
    for stage, part in enumerate(own):
        window = {d: later(part, d) for d in (4, 2, 1)}
        window[0] = part
        window[3] = whole
        windows.append([window[d] for d in range(BACK, -1, -1)])
        if stage == 0:
            late = lax.optimization_barrier((*late, *early, part))[:2]
            late = [swap(late[0], 2), swap(late[1], 6)]
    lanes = GQ * (ROWS + BSLOT)
    rows, sums, partial = None, {}, {}
    for first, count, part in CALLS:
        stage, row_at, (sum_first, sum_count) = part, 0, SUMS[part]
        here = pack((0, 2), first, count, order if rows is None else rows[0])
        operands = [x, dense, back, vec, here[0], *(late if stage else early), here[1], *windows[stage]]
        fixed = len(operands)
        aliases, outputs = {}, 0
        for begun, size in ((rows, 6), (sums.get(part), 2)):
            for i, array in enumerate(begun or ()):
                aliases[len(operands)] = outputs + i
                operands.append(array)
            outputs += size
        result = pl.pallas_call(
            attend,
            grid=(count,),
            out_shape=[shape(2 * CAP, KVH * WIDE)] * 2
            + [shape(2 * CAP, KVH * WIDE // 2)] * 4
            + [shape(8 * ROWS, sum_count * 2 * HD), shape(2 * ROWS, sum_count * 2 * HD)],
            in_specs=[SMEM, full(2 * ROWS, 384), full(6 * CAP, ROWS), full(8, ROWS)]
            + [columns(2 * MSG, WIDE, at) for at in (row_at,) * 4]
            + [columns(2 * ROWS, 2 * HD, first if d == 3 else row_at) for d in range(BACK, -1, -1)]
            + [pl.BlockSpec(memory_space=pl.ANY)] * (len(operands) - fixed),
            out_specs=[columns(2 * CAP, WIDE, first)] * 2
            + [columns(2 * CAP, WIDE // 2, first)] * 4
            + [columns(r * ROWS, 2 * HD, first - sum_first) for r in (8, 2)],
            input_output_aliases=aliases,
            scratch_shapes=[
                pltpu.VMEM((2, WIN, 2 * ROWS), f32),
                pltpu.VMEM((lanes, HD), bf16),
                pltpu.VMEM((lanes, HD), bf16),
                pltpu.VMEM((HD, lanes), bf16),
                pltpu.VMEM((WIN, HD), bf16),
                pltpu.VMEM((WIN, HD), bf16),
                pltpu.VMEM((HD, WIN), bf16),
                pltpu.VMEM((WIN, HD), f32),
                pltpu.VMEM((WIN, HD), f32),
            ],
            compiler_params=params(60),
            cost_estimate=cost(count * lanes * WIN * HD * 2 * 10, 8 << 20, count * lanes * WIN),
            name="attend",
        )(*operands)
        rows, sums[part] = result[:6], result[6:]
        if first + count == sum_first + sum_count:
            terms, far = sums[part]
            rings = [[4 * z + i for i in range(4)] for z in range(seq_count // 4)]
            terms = lax.all_to_all(
                terms, "seq", split_axis=0, concat_axis=0, axis_index_groups=rings, tiled=True
            )
            partial[part] = [terms, far]

    rests = []
    for part, (_, count) in enumerate(SUMS):
        terms, far = partial[part]
        terms, _ = lax.optimization_barrier((terms, partial[len(SUMS) - 1][1]))
        rest = pl.pallas_call(
            pass_on,
            out_shape=shape(2 * ROWS, count * 2 * HD),
            in_specs=[SMEM] + [pl.BlockSpec(memory_space=pltpu.VMEM)] * 2,
            compiler_params=params(32),
            cost_estimate=cost(1e6, 2 << 20),
            name="pass_on",
        )(x, terms, far)
        rests.append(earlier(rest, BACK))
        partial[part] = [terms, rests[part]]
    gradients = [rows[0]]
    for k, piece in zip((1,) + NEAR, rows[1:]):
        if k in (3, 7):
            piece, _ = lax.optimization_barrier((piece, rests[0]))
        gradients.append(swap(piece, k))

    spread, _ = lax.optimization_barrier((spread, gradients[1:]))
    message = pl.pallas_call(
        return_keys,
        out_shape=shape(GROUPS * MSG, wide),
        compiler_params=params(32),
        in_specs=[SMEM] + [pl.BlockSpec(memory_space=pltpu.VMEM)] * (1 + 2 * len(SUMS)),
        cost_estimate=cost(1e8, 3 << 20),
        name="return_keys",
    )(x, spread, *partial[0], *partial[1])
    message = lax.all_to_all(message, "grp", split_axis=0, concat_axis=0, tiled=True)

    grad_query = pl.pallas_call(
        unpack_rows,
        grid=(KVH,),
        out_shape=shape(ROWS, KVH * WIDE),
        in_specs=[full(ROWS, PAIR)] + [columns(2 * CAP, WIDE)] * 2 + [columns(2 * CAP, WIDE // 2)] * 4,
        out_specs=columns(ROWS, WIDE),
        compiler_params=params(60),
        cost_estimate=cost(4e8, 6 << 20),
        name="unpack_rows",
    )(order, *gradients)

    grad_key, grad_value = pl.pallas_call(
        unpack_keys,
        out_shape=[shape(ROWS, KVH * HD)] * 2,
        compiler_params=params(32),
        cost_estimate=cost(1e8, 1 << 20),
        name="unpack_keys",
    )(sort, message)
    return (grad_query, grad_key, grad_value)


def solution(mesh):
    in_specs = (
        P(("grp", "seq"), None),
        P(("grp", "seq"), None),
        P(("grp", "seq"), None),
        P(("grp", "seq"), None),
        P(("grp", "seq")),
        P("grp", None),
    )
    out_specs = (P(("grp", "seq"), None), P(("grp", "seq"), None), P(("grp", "seq"), None))
    return jax.shard_map(
        on_device, mesh=mesh, in_specs=in_specs, out_specs=out_specs, check_vma=False
    )
```

profile of v0, /device:TPU:1, one launch (start us, length us, event | category | flops | bytes accessed | tf_op | source)
XLA Modules:
  0.0 168.2 jit_solution(8744587682865715031)
XLA Ops:
  0.6 3.3 %collective-permute-start.1 = (bf16[128,8192]{1,0:T(8,128)(2,1)}, bf16[128,8192]{1,0:T(8,128)(2,1)}, u32[]{:S(2)}, u32[]{:S(2)}) collective-permute-start(bf16[128,8192]{1,0:T(8,128)(2,1)} %query_ref.7), channel_id=1, source_target_pairs={{0,32},{32,0},{64,96},{96,64},{128,160},{160,128},{192,224},{224,1... | collective-permute-start | bytes 6291464 | tf_op jit(solution)/shard_map/ppermute | solution.py:336
  4.1 0.8 copy.15.col_ref
  4.8 0.6 copy-done.3
  5.5 0.9 copy-done.8
  6.4 0.9 copy-done.9
  7.3 0.7 copy-done.12
  8.0 2.0 %pack_keys.1 = (bf16[384,1152]{1,0:T(8,128)(2,1)}, bf16[128,256]{1,0:T(8,128)(2,1)S(1)}, bf16[128,384]{1,0:T(8,128)(2,1)S(1)}) custom-call(s32[1]{0:T(128)} %bitcast.me_ref, s32[16]{0:T(128)S(1)} %bitcast.26, s32[1,128]{1,0:T(1,128)S(1)} %bitcast.25, s32[128,1]{1,0:T(8,128)S(1)} %copy.15.col_ref, bf16[128,512]{1,0:T(8,128)(2,1)S(1)} %copy-done.8, ...), custom_call_target="tpu_custom_call" | custom-call | flops 100000000 | bytes 1048576 | tf_op jit(solution)/shard_map/pack_keys/pallas_call | solution.py:345
  9.9 0.6 copy-done
  10.5 3.9 %all-to-all-start = ((bf16[8,48,1152]{2,1,0:T(8,128)(2,1)}), bf16[8,48,1152]{2,1,0:T(8,128)(2,1)S(1)}, u32[]{:S(2)}, u32[]{:S(2)}) async-start(bf16[8,48,1152]{2,1,0:T(8,128)(2,1)} %bitcast.6), calls=%async_computation | async-start | bytes 1769472 | tf_op jit(solution)/shard_map/all_to_all | solution.py:357
  14.6 0.9 collective-permute-done
  15.5 0.6 copy-done.14
  16.1 4.9 %pack_rows.5 = (bf16[96,4096]{1,0:T(8,128)(2,1)}, bf16[96,4096]{1,0:T(8,128)(2,1)}) custom-call(s32[1]{0:T(128)} %bitcast.me_ref, s32[1,128]{1,0:T(1,128)} %bitcast.21, s32[1,128]{1,0:T(1,128)} %bitcast.29, bf16[128,8192]{1,0:T(8,128)(2,1)} %query_ref.7, bf16[128,8192]{1,0:T(8,128)(2,1)} %grad_ref.7, ...), custom_call_target="tpu_custom_call" | custom-call | flops 200000000 | bytes 4194304 | tf_op jit(solution)/shard_map/pack_rows/pallas_call | solution.py:363
  21.0 5.0 %pack_rows.4 = (bf16[96,4096]{1,0:T(8,128)(2,1)}, bf16[96,4096]{1,0:T(8,128)(2,1)}) custom-call(s32[1]{0:T(128)} %bitcast.me_ref, s32[1,128]{1,0:T(1,128)} %bitcast.22, s32[1,128]{1,0:T(1,128)} %bitcast.30, bf16[128,8192]{1,0:T(8,128)(2,1)} %query_ref.7, bf16[128,8192]{1,0:T(8,128)(2,1)} %grad_ref.7, ...), custom_call_target="tpu_custom_call" | custom-call | flops 200000000 | bytes 4194304 | tf_op jit(solution)/shard_map/pack_rows/pallas_call | solution.py:363
  25.9 1.8 %all-to-all-done = bf16[8,48,1152]{2,1,0:T(8,128)(2,1)S(1)} async-done(((bf16[8,48,1152]{2,1,0:T(8,128)(2,1)}), bf16[8,48,1152]{2,1,0:T(8,128)(2,1)S(1)}, u32[]{:S(2)}, u32[]{:S(2)}) %all-to-all-start) | async-done | bytes 884768 | tf_op jit(solution)/shard_map/all_to_all | solution.py:357
  28.1 1.2 collective-permute-start.4
  29.3 0.9 group_keys.1
  30.3 1.8 %collective-permute-start.6 = (bf16[256,1024]{1,0:T(8,128)(2,1)S(1)}, bf16[256,1024]{1,0:T(8,128)(2,1)S(1)}, u32[]{:S(2)}, u32[]{:S(2)}) collective-permute-start(bf16[256,1024]{1,0:T(8,128)(2,1)S(1)} %get-tuple-element.66), channel_id=1, source_target_pairs={{0,3},{1,4},{2,5},{3,6},{4,7},{5,8},{6,9},{7,10},{8,11},{9,12},{10... | collective-permute-start | bytes 1572872 | tf_op jit(solution)/shard_map/ppermute | solution.py:339
  32.1 1.6 collective-permute-start.5
  33.7 1.9 %collective-permute-start.7 = (bf16[256,512]{1,0:T(8,128)(2,1)S(1)}, bf16[256,512]{1,0:T(8,128)(2,1)S(1)}, u32[]{:S(2)}, u32[]{:S(2)}) collective-permute-start(bf16[256,512]{1,0:T(8,128)(2,1)S(1)} %get-tuple-element.65.refs_8_), channel_id=1, source_target_pairs={{0,2},{1,3},{2,4},{3,5},{4,6},{5,7},{6,8},{7,9},{8,10},{9,11},{10,... | collective-permute-start | bytes 786440 | tf_op jit(solution)/shard_map/ppermute | solution.py:339
  35.6 10.7 %collective-permute-done.3.refs_1_ = bf16[96,4096]{1,0:T(8,128)(2,1)S(1)} collective-permute-done((bf16[96,4096]{1,0:T(8,128)(2,1)}, bf16[96,4096]{1,0:T(8,128)(2,1)S(1)}, u32[]{:S(2)}, u32[]{:S(2)}) %collective-permute-start.3) | collective-permute-done | bytes 786464 | tf_op jit(solution)/shard_map/ppermute | solution.py:336
  46.3 0.5 collective-permute-start.8
  47.2 5.0 %pack_rows.6 = (bf16[96,4096]{1,0:T(8,128)(2,1)}, bf16[96,4096]{1,0:T(8,128)(2,1)}) custom-call(s32[1]{0:T(128)} %bitcast.me_ref, s32[1,128]{1,0:T(1,128)} %bitcast.23, s32[1,128]{1,0:T(1,128)} %bitcast.31, bf16[128,8192]{1,0:T(8,128)(2,1)} %query_ref.7, bf16[128,8192]{1,0:T(8,128)(2,1)} %grad_ref.7, ...), custom_call_target="tpu_custom_call" | custom-call | flops 200000000 | bytes 4194304 | tf_op jit(solution)/shard_map/pack_rows/pallas_call | solution.py:363
  52.2 1.3 collective-permute-start.11
  53.5 2.4 %collective-permute-start.12 = (bf16[256,512]{1,0:T(8,128)(2,1)S(1)}, bf16[256,512]{1,0:T(8,128)(2,1)}, u32[]{:S(2)}, u32[]{:S(2)}) collective-permute-start(bf16[256,512]{1,0:T(8,128)(2,1)S(1)} %get-tuple-element.74.refs_8_), channel_id=1, source_target_pairs={{0,2},{1,3},{2,4},{3,5},{4,6},{5,7},{6,8},{7,9},{8,10},{9,11},{10,... | collective-permute-start | bytes 786440 | tf_op jit(solution)/shard_map/ppermute | solution.py:339
  56.0 4.4 %collective-permute-done.7.refs_6_ = bf16[256,512]{1,0:T(8,128)(2,1)S(1)} collective-permute-done((bf16[256,512]{1,0:T(8,128)(2,1)S(1)}, bf16[256,512]{1,0:T(8,128)(2,1)S(1)}, u32[]{:S(2)}, u32[]{:S(2)}) %collective-permute-start.7) | collective-permute-done | bytes 262176 | tf_op jit(solution)/shard_map/ppermute | solution.py:339
  60.6 5.4 %collective-permute-done.8.refs_7_ = bf16[256,512]{1,0:T(8,128)(2,1)S(1)} collective-permute-done((bf16[256,512]{1,0:T(8,128)(2,1)S(1)}, bf16[256,512]{1,0:T(8,128)(2,1)S(1)}, u32[]{:S(2)}, u32[]{:S(2)}) %collective-permute-start.8) | collective-permute-done | bytes 262176 | tf_op jit(solution)/shard_map/ppermute | solution.py:339
  66.0 0.7 collective-permute-start.10
  67.5 20.0 %attend.2 = (bf16[48,8192]{1,0:T(8,128)(2,1)}, bf16[48,8192]{1,0:T(8,128)(2,1)}, bf16[48,4096]{1,0:T(8,128)(2,1)}, bf16[48,4096]{1,0:T(8,128)(2,1)}, bf16[48,409...) custom-call(s32[1]{0:T(128)S(6)} %and.5.x_ref, ...), custom_call_target="tpu_custom_call" | custom-call | flops 10066329600 | bytes 8388608 | tf_op jit(solution)/shard_map/attend/pallas_call | solution.py:425
  87.5 3.5 %all-to-all-start.1 = ((bf16[4,256,512]{2,1,0:T(8,128)(2,1)}), bf16[4,256,512]{2,1,0:T(8,128)(2,1)S(1)}, u32[]{:S(2)}, u32[]{:S(2)}) async-start(bf16[4,256,512]{2,1,0:T(8,128)(2,1)} %bitcast.27), calls=%async_computation.1 | async-start | bytes 2097152 | tf_op jit(solution)/shard_map/all_to_all | solution.py:458
  91.0 4.9 %pack_rows.7 = (bf16[96,4096]{1,0:T(8,128)(2,1)}, bf16[96,4096]{1,0:T(8,128)(2,1)}) custom-call(s32[1]{0:T(128)} %bitcast.me_ref, s32[1,128]{1,0:T(1,128)} %bitcast.24, s32[1,128]{1,0:T(1,128)} %bitcast.32, bf16[128,8192]{1,0:T(8,128)(2,1)} %query_ref.7, bf16[128,8192]{1,0:T(8,128)(2,1)} %grad_ref.7, ...), custom_call_target="tpu_custom_call" | custom-call | flops 200000000 | bytes 4194304 | tf_op jit(solution)/shard_map/pack_rows/pallas_call | solution.py:363
  96.0 0.7 copy-done.18
  96.7 20.1 %attend.3 = (bf16[48,8192]{1,0:T(8,128)(2,1)}, bf16[48,8192]{1,0:T(8,128)(2,1)}, bf16[48,4096]{1,0:T(8,128)(2,1)}, bf16[48,4096]{1,0:T(8,128)(2,1)}, bf16[48,409...) custom-call(s32[1]{0:T(128)S(6)} %and.5.x_ref, ...), custom_call_target="tpu_custom_call", output_to_operand_aliasing={{0}: (13, {}), {1}: (14, {}), {2}: (15, {}), {3}: (16, {}),... | custom-call | flops 10066329600 | bytes 8388608 | tf_op jit(solution)/shard_map/attend/pallas_call | solution.py:425
  116.8 4.3 %all-to-all-start.2 = ((bf16[4,256,512]{2,1,0:T(8,128)(2,1)}), bf16[4,256,512]{2,1,0:T(8,128)(2,1)S(1)}, u32[]{:S(2)}, u32[]{:S(2)}) async-start(bf16[4,256,512]{2,1,0:T(8,128)(2,1)} %bitcast.28), calls=%async_computation.2 | async-start | bytes 2097152 | tf_op jit(solution)/shard_map/all_to_all | solution.py:458
  121.1 4.8 %collective-permute-start.14 = (bf16[48,8192]{1,0:T(8,128)(2,1)}, bf16[48,8192]{1,0:T(8,128)(2,1)}, u32[]{:S(2)}, u32[]{:S(2)}) collective-permute-start(bf16[48,8192]{1,0:T(8,128)(2,1)} %get-tuple-element.81), channel_id=1, source_target_pairs={{0,32},{32,0},{64,96},{96,64},{128,160},{160,128},{192,224},{224,1... | collective-permute-start | bytes 2359304 | tf_op jit(solution)/shard_map/ppermute | solution.py:336
  126.2 1.9 %collective-permute-start.16 = (bf16[256,512]{1,0:T(8,128)(2,1)S(1)}, bf16[256,512]{1,0:T(8,128)(2,1)S(1)}, u32[]{:S(2)}, u32[]{:S(2)}) collective-permute-start(bf16[256,512]{1,0:T(8,128)(2,1)S(1)} %pass_on.2), channel_id=1, source_target_pairs={{4,0},{5,1},{6,2},{7,3},{8,4},{9,5},{10,6},{11,7},{12,8},{13,9},{1... | collective-permute-start | bytes 786440 | tf_op jit(solution)/shard_map/ppermute | solution.py:342
  128.1 1.2 collective-permute-start.15
  129.3 0.7 collective-permute-start.18
  130.0 4.1 %collective-permute-done.16.refs_1_ = bf16[256,512]{1,0:T(8,128)(2,1)S(1)} collective-permute-done((bf16[256,512]{1,0:T(8,128)(2,1)S(1)}, bf16[256,512]{1,0:T(8,128)(2,1)S(1)}, u32[]{:S(2)}, u32[]{:S(2)}) %collective-permute-start.16) | collective-permute-done | bytes 262176 | tf_op jit(solution)/shard_map/ppermute | solution.py:342
  134.2 1.5 collective-permute-start.19
  136.3 2.5 %collective-permute-done.15.refs_0_ = bf16[48,4096]{1,0:T(8,128)(2,1)S(1)} collective-permute-done((bf16[48,4096]{1,0:T(8,128)(2,1)}, bf16[48,4096]{1,0:T(8,128)(2,1)S(1)}, u32[]{:S(2)}, u32[]{:S(2)}) %collective-permute-start.15) | collective-permute-done | bytes 393248 | tf_op jit(solution)/shard_map/ppermute | solution.py:336
  138.8 0.7 collective-permute-start.20
  139.5 1.4 collective-permute-done.18.refs_2_
  140.9 9.2 %collective-permute-done.19.refs_3_ = bf16[48,4096]{1,0:T(8,128)(2,1)} collective-permute-done((bf16[48,4096]{1,0:T(8,128)(2,1)}, bf16[48,4096]{1,0:T(8,128)(2,1)}, u32[]{:S(2)}, u32[]{:S(2)}) %collective-permute-start.19) | collective-permute-done | bytes 393248 | tf_op jit(solution)/shard_map/ppermute | solution.py:336
  150.1 1.7 %return_keys.1 = bf16[384,1024]{1,0:T(8,128)(2,1)} custom-call(s32[1]{0:T(128)S(6)} %and.5.x_ref, bf16[768,128]{1,0:T(8,128)(2,1)S(1)} %get-tuple-element.94.spread_ref, bf16[1024,512]{1,0:T(8,128)(2,1)S(1)} %bitcast.15, bf16[256,512]{1,0:T(8,128)(2,1)S(1)} %collective-permute-done.16.refs_1_, bf16[1024,512]{1,0:T(8,128)(2,1)S(1)} %bitcast.17, ...), custom_call_target="tpu_custom_call" | custom-call | flops 100000000 | bytes 3145728 | tf_op jit(solution)/shard_map/return_keys/pallas_call | solution.py:484
  151.8 3.5 %all-to-all-start.3 = ((bf16[8,48,1024]{2,1,0:T(8,128)(2,1)}), bf16[8,48,1024]{2,1,0:T(8,128)(2,1)S(1)}, u32[]{:S(2)}, u32[]{:S(2)}) async-start(bf16[8,48,1024]{2,1,0:T(8,128)(2,1)} %bitcast.12), calls=%async_computation.3 | async-start | bytes 1572864 | tf_op jit(solution)/shard_map/all_to_all | solution.py:492
  155.3 4.7 %unpack_rows.1 = bf16[128,8192]{1,0:T(8,128)(2,1)} custom-call(bf16[128,256]{1,0:T(8,128)(2,1)} %copy-done, bf16[48,8192]{1,0:T(8,128)(2,1)} %get-tuple-element.80.own_ref, bf16[48,8192]{1,0:T(8,128)(2,1)} %collective-permute-done.14.core_ref, bf16[48,4096]{1,0:T(8,128)(2,1)} %copy-done.13, bf16[48,4096]{1,0:T(8,128)(2,1)} %collective-permute-done.17.refs_1_, ...), custom_call_target="tpu_custom_call" | custom-call | flops 400000000 | bytes 6291456 | tf_op jit(solution)/shard_map/unpack_rows/pallas_call | solution.py:494
  160.0 7.2 %all-to-all-done.3 = bf16[8,48,1024]{2,1,0:T(8,128)(2,1)S(1)} async-done(((bf16[8,48,1024]{2,1,0:T(8,128)(2,1)}), bf16[8,48,1024]{2,1,0:T(8,128)(2,1)S(1)}, u32[]{:S(2)}, u32[]{:S(2)}) %all-to-all-start.3) | async-done | bytes 786464 | tf_op jit(solution)/shard_map/all_to_all | solution.py:492
  167.2 1.0 unpack_keys.1
  (60 shorter events, 3.1 us)
Async XLA Ops:
  0.6 13.8 %copy-start.4 = (s32[128]{0:T(128)S(1)}, s32[128]{0:T(128)}, u32[]{:S(2)}) copy-start(s32[128]{0:T(128)} %param.10) | copy-start | bytes 1540
  0.6 14.9 %collective-permute-start.1 = (bf16[128,8192]{1,0:T(8,128)(2,1)}, bf16[128,8192]{1,0:T(8,128)(2,1)}, u32[]{:S(2)}, u32[]{:S(2)}) collective-permute-start(bf16[128,8192]{1,0:T(8,128)(2,1)} %query_ref.7), channel_id=1, source_target_pairs={{0,32},{32,0},{64,96},{96,64},{128,160},{160,128},{192,224},{224,1... | collective-permute-start | bytes 6291464 | tf_op jit(solution)/shard_map/ppermute | solution.py:336
  4.0 11.6 %collective-permute-start.2 = (bf16[128,8192]{1,0:T(8,128)(2,1)}, bf16[128,8192]{1,0:T(8,128)(2,1)}, u32[]{:S(2)}, u32[]{:S(2)}) collective-permute-start(bf16[128,8192]{1,0:T(8,128)(2,1)} %grad_ref.7), channel_id=1, source_target_pairs={{0,32},{32,0},{64,96},{96,64},{128,160},{160,128},{192,224},{224,1... | collective-permute-start | bytes 6291464 | tf_op jit(solution)/shard_map/ppermute | solution.py:336
  4.8 0.7 copy-start.3
  5.5 0.9 copy-start.8
  6.4 0.9 copy-start.9
  7.3 0.7 copy-start.12
  9.9 0.6 copy-start
  10.5 17.2 %all-to-all-start = ((bf16[8,48,1152]{2,1,0:T(8,128)(2,1)}), bf16[8,48,1152]{2,1,0:T(8,128)(2,1)S(1)}, u32[]{:S(2)}, u32[]{:S(2)}) async-start(bf16[8,48,1152]{2,1,0:T(8,128)(2,1)} %bitcast.6), calls=%async_computation | async-start | bytes 1769472 | tf_op jit(solution)/shard_map/all_to_all | solution.py:357
  14.4 1.1 collective-permute-start
  15.5 0.6 copy-start.14
  27.8 18.5 %collective-permute-start.3 = (bf16[96,4096]{1,0:T(8,128)(2,1)}, bf16[96,4096]{1,0:T(8,128)(2,1)S(1)}, u32[]{:S(2)}, u32[]{:S(2)}) collective-permute-start(bf16[96,4096]{1,0:T(8,128)(2,1)} %get-tuple-element.62), channel_id=1, source_target_pairs={{0,64},{32,96},{64,0},{96,32},{128,192},{160,224},{192,128},{224,1... | collective-permute-start | bytes 2359304 | tf_op jit(solution)/shard_map/ppermute | solution.py:336
  28.1 24.1 %collective-permute-start.4 = (bf16[96,4096]{1,0:T(8,128)(2,1)}, bf16[96,4096]{1,0:T(8,128)(2,1)}, u32[]{:S(2)}, u32[]{:S(2)}) collective-permute-start(bf16[96,4096]{1,0:T(8,128)(2,1)} %get-tuple-element.63), channel_id=1, source_target_pairs={{0,192},{32,224},{64,128},{96,160},{128,64},{160,96},{192,0},{224,... | collective-permute-start | bytes 2359304 | tf_op jit(solution)/shard_map/ppermute | solution.py:336
  30.2 21.9 %copy-start.6 = (bf16[256,512]{1,0:T(8,128)(2,1)}, bf16[256,512]{1,0:T(8,128)(2,1)S(1)}, u32[]{:S(2)}) copy-start(bf16[256,512]{1,0:T(8,128)(2,1)S(1)} %get-tuple-element.65.refs_8_) | copy-start | bytes 786436
  30.2 21.9 %copy-start.7 = (bf16[256,384]{1,0:T(8,128)(2,1)}, bf16[256,384]{1,0:T(8,128)(2,1)S(1)}, u32[]{:S(2)}) copy-start(bf16[256,384]{1,0:T(8,128)(2,1)S(1)} %get-tuple-element.58.dense_ref) | copy-start | bytes 589828
  30.2 21.9 %copy-start.10 = (bf16[144,128]{1,0:T(8,128)(2,1)}, bf16[144,128]{1,0:T(8,128)(2,1)S(1)}, u32[]{:S(2)}) copy-start(bf16[144,128]{1,0:T(8,128)(2,1)S(1)} %get-tuple-element.59.back_ref) | copy-start | bytes 110596
  30.3 21.9 %copy-start.11 = (s32[8,128]{1,0:T(8,128)}, s32[8,128]{1,0:T(8,128)S(1)}, u32[]{:S(2)}) copy-start(s32[8,128]{1,0:T(8,128)S(1)} %get-tuple-element.60.vec_ref) | copy-start | bytes 12292
  30.3 30.1 %copy-start.5 = (bf16[256,512]{1,0:T(8,128)(2,1)}, bf16[256,512]{1,0:T(8,128)(2,1)S(1)}, u32[]{:S(2)}) copy-start(bf16[256,512]{1,0:T(8,128)(2,1)S(1)} %get-tuple-element.74.refs_8_) | copy-start | bytes 786436
  30.3 36.4 %collective-permute-start.6 = (bf16[256,1024]{1,0:T(8,128)(2,1)S(1)}, bf16[256,1024]{1,0:T(8,128)(2,1)S(1)}, u32[]{:S(2)}, u32[]{:S(2)}) collective-permute-start(bf16[256,1024]{1,0:T(8,128)(2,1)S(1)} %get-tuple-element.66), channel_id=1, source_target_pairs={{0,3},{1,4},{2,5},{3,6},{4,7},{5,8},{6,9},{7,10},{8,11},{9,12},{10... | collective-permute-start | bytes 1572872 | tf_op jit(solution)/shard_map/ppermute | solution.py:339
  32.1 21.4 %collective-permute-start.5 = (bf16[256,512]{1,0:T(8,128)(2,1)S(1)}, bf16[256,512]{1,0:T(8,128)(2,1)S(1)}, u32[]{:S(2)}, u32[]{:S(2)}) collective-permute-start(bf16[256,512]{1,0:T(8,128)(2,1)S(1)} %get-tuple-element.65.refs_8_), channel_id=1, source_target_pairs={{0,4},{1,5},{2,6},{3,7},{4,8},{5,9},{6,10},{7,11},{8,12},{9,13},{1... | collective-permute-start | bytes 786440 | tf_op jit(solution)/shard_map/ppermute | solution.py:339
  33.7 26.6 %collective-permute-start.7 = (bf16[256,512]{1,0:T(8,128)(2,1)S(1)}, bf16[256,512]{1,0:T(8,128)(2,1)S(1)}, u32[]{:S(2)}, u32[]{:S(2)}) collective-permute-start(bf16[256,512]{1,0:T(8,128)(2,1)S(1)} %get-tuple-element.65.refs_8_), channel_id=1, source_target_pairs={{0,2},{1,3},{2,4},{3,5},{4,6},{5,7},{6,8},{7,9},{8,10},{9,11},{10,... | collective-permute-start | bytes 786440 | tf_op jit(solution)/shard_map/ppermute | solution.py:339
  46.3 0.9 copy-start.16
  46.3 19.7 %collective-permute-start.8 = (bf16[256,512]{1,0:T(8,128)(2,1)S(1)}, bf16[256,512]{1,0:T(8,128)(2,1)S(1)}, u32[]{:S(2)}, u32[]{:S(2)}) collective-permute-start(bf16[256,512]{1,0:T(8,128)(2,1)S(1)} %get-tuple-element.65.refs_8_), channel_id=1, source_target_pairs={{0,1},{1,2},{2,3},{3,4},{4,5},{5,6},{6,7},{7,8},{8,9},{9,10},{10,1... | collective-permute-start | bytes 786440 | tf_op jit(solution)/shard_map/ppermute | solution.py:339
  47.2 19.5 %copy-start.15 = (bf16[96,4096]{1,0:T(8,128)(2,1)S(1)}, bf16[96,4096]{1,0:T(8,128)(2,1)}, u32[]{:S(2)}) copy-start(bf16[96,4096]{1,0:T(8,128)(2,1)} %get-tuple-element.71) | copy-start | bytes 2359300
  52.2 43.8 %collective-permute-start.11 = (bf16[256,512]{1,0:T(8,128)(2,1)S(1)}, bf16[256,512]{1,0:T(8,128)(2,1)S(1)}, u32[]{:S(2)}, u32[]{:S(2)}) collective-permute-start(bf16[256,512]{1,0:T(8,128)(2,1)S(1)} %get-tuple-element.74.refs_8_), channel_id=1, source_target_pairs={{0,4},{1,5},{2,6},{3,7},{4,8},{5,9},{6,10},{7,11},{8,12},{9,13},{1... | collective-permute-start | bytes 786440 | tf_op jit(solution)/shard_map/ppermute | solution.py:339
  53.5 13.5 %copy-start.19 = (bf16[256,512]{1,0:T(8,128)(2,1)}, bf16[256,512]{1,0:T(8,128)(2,1)S(1)}, u32[]{:S(2)}) copy-start(bf16[256,512]{1,0:T(8,128)(2,1)S(1)} %collective-permute-done.5.refs_4_) | copy-start | bytes 786436
  53.5 42.5 %collective-permute-start.12 = (bf16[256,512]{1,0:T(8,128)(2,1)S(1)}, bf16[256,512]{1,0:T(8,128)(2,1)}, u32[]{:S(2)}, u32[]{:S(2)}) collective-permute-start(bf16[256,512]{1,0:T(8,128)(2,1)S(1)} %get-tuple-element.74.refs_8_), channel_id=1, source_target_pairs={{0,2},{1,3},{2,4},{3,5},{4,6},{5,7},{6,8},{7,9},{8,10},{9,11},{10,... | collective-permute-start | bytes 786440 | tf_op jit(solution)/shard_map/ppermute | solution.py:339
  60.4 6.7 %copy-start.20 = (bf16[256,512]{1,0:T(8,128)(2,1)}, bf16[256,512]{1,0:T(8,128)(2,1)S(1)}, u32[]{:S(2)}) copy-start(bf16[256,512]{1,0:T(8,128)(2,1)S(1)} %collective-permute-done.7.refs_6_) | copy-start | bytes 786436
  60.4 35.6 %collective-permute-start.13 = (bf16[256,512]{1,0:T(8,128)(2,1)S(1)}, bf16[256,512]{1,0:T(8,128)(2,1)}, u32[]{:S(2)}, u32[]{:S(2)}) collective-permute-start(bf16[256,512]{1,0:T(8,128)(2,1)S(1)} %get-tuple-element.74.refs_8_), channel_id=1, source_target_pairs={{0,1},{1,2},{2,3},{3,4},{4,5},{5,6},{6,7},{7,8},{8,9},{9,10},{10,1... | collective-permute-start | bytes 786440 | tf_op jit(solution)/shard_map/ppermute | solution.py:339
  66.0 1.0 copy-start.21
  66.0 30.0 %collective-permute-start.10 = (bf16[96,4096]{1,0:T(8,128)(2,1)}, bf16[96,4096]{1,0:T(8,128)(2,1)}, u32[]{:S(2)}, u32[]{:S(2)}) collective-permute-start(bf16[96,4096]{1,0:T(8,128)(2,1)} %get-tuple-element.72), channel_id=1, source_target_pairs={{0,192},{32,224},{64,128},{96,160},{128,64},{160,96},{192,0},{224,... | collective-permute-start | bytes 2359304 | tf_op jit(solution)/shard_map/ppermute | solution.py:336
  66.7 0.8 copy-start.17
  66.7 29.3 %collective-permute-start.9 = (bf16[96,4096]{1,0:T(8,128)(2,1)S(1)}, bf16[96,4096]{1,0:T(8,128)(2,1)}, u32[]{:S(2)}, u32[]{:S(2)}) collective-permute-start(bf16[96,4096]{1,0:T(8,128)(2,1)S(1)} %copy-done.15), channel_id=1, source_target_pairs={{0,64},{32,96},{64,0},{96,32},{128,192},{160,224},{192,128},{224,1... | collective-permute-start | bytes 2359304 | tf_op jit(solution)/shard_map/ppermute | solution.py:336
  87.5 29.3 %all-to-all-start.1 = ((bf16[4,256,512]{2,1,0:T(8,128)(2,1)}), bf16[4,256,512]{2,1,0:T(8,128)(2,1)S(1)}, u32[]{:S(2)}, u32[]{:S(2)}) async-start(bf16[4,256,512]{2,1,0:T(8,128)(2,1)} %bitcast.27), calls=%async_computation.1 | async-start | bytes 2097152 | tf_op jit(solution)/shard_map/all_to_all | solution.py:458
  95.9 0.7 copy-start.18
  116.7 9.2 %copy-start.1 = (bf16[256,512]{1,0:T(8,128)(2,1)S(1)}, bf16[256,512]{1,0:T(8,128)(2,1)}, u32[]{:S(2)}) copy-start(bf16[256,512]{1,0:T(8,128)(2,1)} %get-tuple-element.87.far_ref) | copy-start | bytes 786436
  116.8 19.3 %copy-start.2 = (bf16[256,512]{1,0:T(8,128)(2,1)S(1)}, bf16[256,512]{1,0:T(8,128)(2,1)}, u32[]{:S(2)}) copy-start(bf16[256,512]{1,0:T(8,128)(2,1)} %get-tuple-element.85.far_ref) | copy-start | bytes 786436
  116.8 19.3 %all-to-all-start.2 = ((bf16[4,256,512]{2,1,0:T(8,128)(2,1)}), bf16[4,256,512]{2,1,0:T(8,128)(2,1)S(1)}, u32[]{:S(2)}, u32[]{:S(2)}) async-start(bf16[4,256,512]{2,1,0:T(8,128)(2,1)} %bitcast.28), calls=%async_computation.2 | async-start | bytes 2097152 | tf_op jit(solution)/shard_map/all_to_all | solution.py:458
  121.1 29.0 %collective-permute-start.14 = (bf16[48,8192]{1,0:T(8,128)(2,1)}, bf16[48,8192]{1,0:T(8,128)(2,1)}, u32[]{:S(2)}, u32[]{:S(2)}) collective-permute-start(bf16[48,8192]{1,0:T(8,128)(2,1)} %get-tuple-element.81), channel_id=1, source_target_pairs={{0,32},{32,0},{64,96},{96,64},{128,160},{160,128},{192,224},{224,1... | collective-permute-start | bytes 2359304 | tf_op jit(solution)/shard_map/ppermute | solution.py:336
  126.2 8.0 %collective-permute-start.16 = (bf16[256,512]{1,0:T(8,128)(2,1)S(1)}, bf16[256,512]{1,0:T(8,128)(2,1)S(1)}, u32[]{:S(2)}, u32[]{:S(2)}) collective-permute-start(bf16[256,512]{1,0:T(8,128)(2,1)S(1)} %pass_on.2), channel_id=1, source_target_pairs={{4,0},{5,1},{6,2},{7,3},{8,4},{9,5},{10,6},{11,7},{12,8},{13,9},{1... | collective-permute-start | bytes 786440 | tf_op jit(solution)/shard_map/ppermute | solution.py:342
  128.1 10.7 %collective-permute-start.15 = (bf16[48,4096]{1,0:T(8,128)(2,1)}, bf16[48,4096]{1,0:T(8,128)(2,1)S(1)}, u32[]{:S(2)}, u32[]{:S(2)}) collective-permute-start(bf16[48,4096]{1,0:T(8,128)(2,1)} %get-tuple-element.82), channel_id=1, source_target_pairs={{0,64},{32,96},{64,0},{96,32},{128,192},{160,224},{192,128},{224,1... | collective-permute-start | bytes 1179656 | tf_op jit(solution)/shard_map/ppermute | solution.py:336
  129.3 11.6 %collective-permute-start.18 = (bf16[48,4096]{1,0:T(8,128)(2,1)}, bf16[48,4096]{1,0:T(8,128)(2,1)}, u32[]{:S(2)}, u32[]{:S(2)}) collective-permute-start(bf16[48,4096]{1,0:T(8,128)(2,1)} %get-tuple-element.89), channel_id=1, source_target_pairs={{0,192},{32,224},{64,128},{96,160},{128,64},{160,96},{192,0},{224,... | collective-permute-start | bytes 1179656 | tf_op jit(solution)/shard_map/ppermute | solution.py:336
  134.2 15.9 %collective-permute-start.19 = (bf16[48,4096]{1,0:T(8,128)(2,1)}, bf16[48,4096]{1,0:T(8,128)(2,1)}, u32[]{:S(2)}, u32[]{:S(2)}) collective-permute-start(bf16[48,4096]{1,0:T(8,128)(2,1)} %get-tuple-element.91), channel_id=1, source_target_pairs={{0,224},{32,192},{64,160},{96,128},{128,96},{160,64},{192,32},{224... | collective-permute-start | bytes 1179656 | tf_op jit(solution)/shard_map/ppermute | solution.py:336
  135.7 14.4 %collective-permute-start.17 = (bf16[48,4096]{1,0:T(8,128)(2,1)}, bf16[48,4096]{1,0:T(8,128)(2,1)}, u32[]{:S(2)}, u32[]{:S(2)}) collective-permute-start(bf16[48,4096]{1,0:T(8,128)(2,1)} %get-tuple-element.88), channel_id=1, source_target_pairs={{0,96},{32,64},{64,32},{96,0},{128,224},{160,192},{192,160},{224,1... | collective-permute-start | bytes 1179656 | tf_op jit(solution)/shard_map/ppermute | solution.py:336
  138.8 13.0 %copy-start.13 = (bf16[48,4096]{1,0:T(8,128)(2,1)}, bf16[48,4096]{1,0:T(8,128)(2,1)S(1)}, u32[]{:S(2)}) copy-start(bf16[48,4096]{1,0:T(8,128)(2,1)S(1)} %collective-permute-done.15.refs_0_) | copy-start | bytes 1179652
  138.8 11.3 %collective-permute-start.20 = (bf16[256,512]{1,0:T(8,128)(2,1)S(1)}, bf16[256,512]{1,0:T(8,128)(2,1)S(1)}, u32[]{:S(2)}, u32[]{:S(2)}) collective-permute-start(bf16[256,512]{1,0:T(8,128)(2,1)S(1)} %pass_on.3), channel_id=1, source_target_pairs={{4,0},{5,1},{6,2},{7,3},{8,4},{9,5},{10,6},{11,7},{12,8},{13,9},{1... | collective-permute-start | bytes 786440 | tf_op jit(solution)/shard_map/ppermute | solution.py:342
  151.8 15.4 %all-to-all-start.3 = ((bf16[8,48,1024]{2,1,0:T(8,128)(2,1)}), bf16[8,48,1024]{2,1,0:T(8,128)(2,1)S(1)}, u32[]{:S(2)}, u32[]{:S(2)}) async-start(bf16[8,48,1024]{2,1,0:T(8,128)(2,1)} %bitcast.12), calls=%async_computation.3 | async-start | bytes 1572864 | tf_op jit(solution)/shard_map/all_to_all | solution.py:492
where the time goes:
time: 169 us; the launch traced here: 168 us
  Pallas kernels  70.6 us (42%)
  waiting for transfers between devices  47.6 us (28%)
  starting transfers between devices  42.5 us (25%)
  local copies, waits for them, and re-layouts  6.68 us (4%)
    pallas_call x2, Pallas kernels, on_device(): pl.pallas_call(attend, grid=(count,), out_shape=[shape(2 * CAP, KVH * WID...  40.1 us
    ppermute x12, waiting for transfers between devices, swap(): return lax.ppermute(tensor, 'grp', [(i, i ^ k) for i in range(GROUPS)])  24.6 us
    pallas_call x4, Pallas kernels, pack(): pl.pallas_call(functools.partial(pack_rows, blocks), grid=(count * WIDE /...  19.7 us
    ppermute x12, starting transfers between devices, swap(): return lax.ppermute(tensor, 'grp', [(i, i ^ k) for i in range(GROUPS)])  14.9 us
    ppermute x7, starting transfers between devices, later(): lax.ppermute(tensor, 'seq', [(i, (i + distance) % seq_count) for i in ran...  9.82 us
    ppermute x7, waiting for transfers between devices, later(): lax.ppermute(tensor, 'seq', [(i, (i + distance) % seq_count) for i in ran...  9.8 us
    all_to_all x2, waiting for transfers between devices, on_device(): lax.all_to_all(message, 'grp', split_axis=0, concat_axis=0, tiled=True)  8.98 us
    all_to_all x2, starting transfers between devices, on_device(): lax.all_to_all(terms, 'seq', split_axis=0, concat_axis=0, axis_index_grou...  7.84 us
  transfers between devices with their start and end apart: 25, of which 10 were waited for; matrix products, arithmetic and copies ran while one was open for 0% of the time, Pallas kernels for 40%

commit v1 on v0

--- a/solution.py
+++ b/solution.py
@@ -400,9 +400,15 @@
 
     x = seq & 3
     whole = later(whole, 3)
+    staying = [pack((0, 2), first, count, order) for first, count, _ in CALLS]
     windows = []
     for stage, part in enumerate(own):
-        window = {d: later(part, d) for d in (4, 2, 1)}
+        window = {d: later(part, d) for d in (4, 2)}
+        held = part
+        if stage == 0:
+            held, *rest = lax.optimization_barrier((part, *staying[0], *staying[1]))
+            staying = [rest[:2], rest[2:]]
+        window[1] = later(held, 1)
         window[0] = part
         window[3] = whole
         windows.append([window[d] for d in range(BACK, -1, -1)])
@@ -413,7 +419,7 @@
     rows, sums, partial = None, {}, {}
     for first, count, part in CALLS:
         stage, row_at, (sum_first, sum_count) = part, 0, SUMS[part]
-        here = pack((0, 2), first, count, order if rows is None else rows[0])
+        here = staying[part]
         operands = [x, dense, back, vec, here[0], *(late if stage else early), here[1], *windows[stage]]
         fixed = len(operands)
         aliases, outputs = {}, 0

time: 169 us -> 166 us (0.982)
  waiting for transfers between devices: 47.6 us -> 35.1 us
  starting transfers between devices: 42.5 us -> 51.8 us
    ppermute x12, waiting for transfers between devices: 24.6 us -> 12.8 us  [swap(): return lax.ppermute(tensor, 'grp', [(i, i ^ k) for i in range(GROUPS)])]
    all_to_all x2, starting transfers between devices: 7.84 us -> 15 us  [on_device(): lax.all_to_all(terms, 'seq', split_axis=0, concat_axis=0, axis_index_grou...]
    ppermute x2, starting transfers between devices: 2.65 us -> 6.41 us  [earlier(): lax.ppermute(tensor, 'seq', [((i + distance) % seq_count, i) for i in ran...]
    ppermute x7, starting transfers between devices: 9.82 us -> 7.74 us  [later(): lax.ppermute(tensor, 'seq', [(i, (i + distance) % seq_count) for i in ran...]
    unnamed x44 -> x46, local copies, waits for them, and re-layouts: 5.92 us -> 5.81 us
  transfers between devices with their start and end apart: 25 -> 25, of which waited for: 10 -> 10; matrix products, arithmetic and copies ran while one was open for 0% -> 0% of each run, Pallas kernels for 40% -> 41%
where the time goes in v1:
time: 166 us; the launch traced here: 165 us
  Pallas kernels  70.6 us (43%)
  starting transfers between devices  51.8 us (31%)
  waiting for transfers between devices  35.1 us (21%)
  local copies, waits for them, and re-layouts  6.57 us (4%)
    pallas_call x2, Pallas kernels, on_device(): pl.pallas_call(attend, grid=(count,), out_shape=[shape(2 * CAP, KVH * WID...  40.1 us
    pallas_call x4, Pallas kernels, pack(): pl.pallas_call(functools.partial(pack_rows, blocks), grid=(count * WIDE /...  19.7 us
    ppermute x12, starting transfers between devices, swap(): return lax.ppermute(tensor, 'grp', [(i, i ^ k) for i in range(GROUPS)])  15.3 us
    all_to_all x2, starting transfers between devices, on_device(): lax.all_to_all(terms, 'seq', split_axis=0, concat_axis=0, axis_index_grou...  15 us
    ppermute x12, waiting for transfers between devices, swap(): return lax.ppermute(tensor, 'grp', [(i, i ^ k) for i in range(GROUPS)])  12.8 us
    ppermute x7, waiting for transfers between devices, later(): lax.ppermute(tensor, 'seq', [(i, (i + distance) % seq_count) for i in ran...  10.1 us
    all_to_all x2, waiting for transfers between devices, on_device(): lax.all_to_all(message, 'grp', split_axis=0, concat_axis=0, tiled=True)  8.75 us
    ppermute x7, starting transfers between devices, later(): lax.ppermute(tensor, 'seq', [(i, (i + distance) % seq_count) for i in ran...  7.74 us
  transfers between devices with their start and end apart: 25, of which 10 were waited for; matrix products, arithmetic and copies ran while one was open for 0% of the time, Pallas kernels for 41%

profile of v1, /device:TPU:1, one launch (start us, length us, event | category | flops | bytes accessed | tf_op | source)
XLA Modules:
  0.0 164.9 jit_solution(9370434874246078810)
XLA Ops:
  0.6 3.3 %collective-permute-start.1 = (bf16[128,8192]{1,0:T(8,128)(2,1)}, bf16[128,8192]{1,0:T(8,128)(2,1)S(1)}, u32[]{:S(2)}, u32[]{:S(2)}) collective-permute-start(bf16[128,8192]{1,0:T(8,128)(2,1)} %query_ref.7), channel_id=1, source_target_pairs={{0,32},{32,0},{64,96},{96,64},{128,160},{160,128},{192,224},{224,1... | collective-permute-start | bytes 6291464 | tf_op jit(solution)/shard_map/ppermute | solution.py:336
  4.1 0.8 copy.15.col_ref
  4.8 0.6 copy-done.3
  5.5 0.9 copy-done.8
  6.4 0.9 copy-done.9
  7.3 0.7 copy-done.12
  8.0 2.0 %pack_keys.1 = (bf16[384,1152]{1,0:T(8,128)(2,1)}, bf16[128,256]{1,0:T(8,128)(2,1)S(1)}, bf16[128,384]{1,0:T(8,128)(2,1)S(1)}) custom-call(s32[1]{0:T(128)} %bitcast.me_ref, s32[16]{0:T(128)S(1)} %bitcast.26, s32[1,128]{1,0:T(1,128)S(1)} %bitcast.25, s32[128,1]{1,0:T(8,128)S(1)} %copy.15.col_ref, bf16[128,512]{1,0:T(8,128)(2,1)S(1)} %copy-done.8, ...), custom_call_target="tpu_custom_call" | custom-call | flops 100000000 | bytes 1048576 | tf_op jit(solution)/shard_map/pack_keys/pallas_call | solution.py:345
  9.9 0.6 copy-done
  10.6 3.9 %all-to-all-start = ((bf16[8,48,1152]{2,1,0:T(8,128)(2,1)}), bf16[8,48,1152]{2,1,0:T(8,128)(2,1)S(1)}, u32[]{:S(2)}, u32[]{:S(2)}) async-start(bf16[8,48,1152]{2,1,0:T(8,128)(2,1)} %bitcast.6), calls=%async_computation | async-start | bytes 1769472 | tf_op jit(solution)/shard_map/all_to_all | solution.py:357
  14.6 0.9 collective-permute-done
  15.6 0.5 copy-done.15
  16.1 0.8 copy-done.13
  16.9 4.8 %pack_rows.5 = (bf16[96,4096]{1,0:T(8,128)(2,1)}, bf16[96,4096]{1,0:T(8,128)(2,1)}) custom-call(s32[1]{0:T(128)} %bitcast.me_ref, s32[1,128]{1,0:T(1,128)} %bitcast.21, s32[1,128]{1,0:T(1,128)} %bitcast.29, bf16[128,8192]{1,0:T(8,128)(2,1)} %query_ref.7, bf16[128,8192]{1,0:T(8,128)(2,1)} %grad_ref.7, bf16[128,8192]{1,0:T(8,128)(2,1)} %copy-done.13, ...), custom_call_target="tpu_custom_call" | custom-call | flops 200000000 | bytes 4194304 | tf_op jit(solution)/shard_map/pack_rows/pallas_call | solution.py:363
  21.7 4.9 %pack_rows.4 = (bf16[96,4096]{1,0:T(8,128)(2,1)}, bf16[96,4096]{1,0:T(8,128)(2,1)}) custom-call(s32[1]{0:T(128)} %bitcast.me_ref, s32[1,128]{1,0:T(1,128)} %bitcast.22, s32[1,128]{1,0:T(1,128)} %bitcast.30, bf16[128,8192]{1,0:T(8,128)(2,1)} %query_ref.7, bf16[128,8192]{1,0:T(8,128)(2,1)} %grad_ref.7, bf16[128,8192]{1,0:T(8,128)(2,1)} %copy-done.13, ...), custom_call_target="tpu_custom_call" | custom-call | flops 200000000 | bytes 4194304 | tf_op jit(solution)/shard_map/pack_rows/pallas_call | solution.py:363
  26.6 1.2 all-to-all-done
  28.1 1.8 %collective-permute-start.4 = (bf16[96,4096]{1,0:T(8,128)(2,1)}, bf16[96,4096]{1,0:T(8,128)(2,1)}, u32[]{:S(2)}, u32[]{:S(2)}) collective-permute-start(bf16[96,4096]{1,0:T(8,128)(2,1)} %get-tuple-element.75), channel_id=1, source_target_pairs={{0,192},{32,224},{64,128},{96,160},{128,64},{160,96},{192,0},{224,... | collective-permute-start | bytes 2359304 | tf_op jit(solution)/shard_map/ppermute | solution.py:336
  29.9 0.9 group_keys.1
  30.9 1.8 %collective-permute-start.8 = (bf16[256,1024]{1,0:T(8,128)(2,1)S(1)}, bf16[256,1024]{1,0:T(8,128)(2,1)}, u32[]{:S(2)}, u32[]{:S(2)}) collective-permute-start(bf16[256,1024]{1,0:T(8,128)(2,1)S(1)} %get-tuple-element.80), channel_id=1, source_target_pairs={{0,3},{1,4},{2,5},{3,6},{4,7},{5,8},{6,9},{7,10},{8,11},{9,12},{10... | collective-permute-start | bytes 1572872 | tf_op jit(solution)/shard_map/ppermute | solution.py:339
  32.7 4.9 %pack_rows.7 = (bf16[96,4096]{1,0:T(8,128)(2,1)}, bf16[96,4096]{1,0:T(8,128)(2,1)}) custom-call(s32[1]{0:T(128)} %bitcast.me_ref, s32[1,128]{1,0:T(1,128)} %bitcast.23, s32[1,128]{1,0:T(1,128)} %bitcast.31, bf16[128,8192]{1,0:T(8,128)(2,1)} %query_ref.7, bf16[128,8192]{1,0:T(8,128)(2,1)} %grad_ref.7, bf16[128,8192]{1,0:T(8,128)(2,1)} %copy-done.13, ...), custom_call_target="tpu_custom_call" | custom-call | flops 200000000 | bytes 4194304 | tf_op jit(solution)/shard_map/pack_rows/pallas_call | solution.py:363
  37.7 5.1 %pack_rows.6 = (bf16[96,4096]{1,0:T(8,128)(2,1)}, bf16[96,4096]{1,0:T(8,128)(2,1)}) custom-call(s32[1]{0:T(128)} %bitcast.me_ref, s32[1,128]{1,0:T(1,128)} %bitcast.24, s32[1,128]{1,0:T(1,128)} %bitcast.32, bf16[128,8192]{1,0:T(8,128)(2,1)} %query_ref.7, bf16[128,8192]{1,0:T(8,128)(2,1)} %grad_ref.7, bf16[128,8192]{1,0:T(8,128)(2,1)} %copy-done.13, ...), custom_call_target="tpu_custom_call" | custom-call | flops 200000000 | bytes 4194304 | tf_op jit(solution)/shard_map/pack_rows/pallas_call | solution.py:363
  43.1 2.7 %collective-permute-start.12 = (bf16[256,512]{1,0:T(8,128)(2,1)S(1)}, bf16[256,512]{1,0:T(8,128)(2,1)S(1)}, u32[]{:S(2)}, u32[]{:S(2)}) collective-permute-start(bf16[256,512]{1,0:T(8,128)(2,1)S(1)} %get-tuple-element.83.refs_8_), channel_id=1, source_target_pairs={{0,2},{1,3},{2,4},{3,5},{4,6},{5,7},{6,8},{7,9},{8,10},{9,11},{10,... | collective-permute-start | bytes 786440 | tf_op jit(solution)/shard_map/ppermute | solution.py:339
  45.9 0.4 collective-permute-done.3.refs_1_
  46.3 1.3 collective-permute-start.11
  47.6 1.5 collective-permute-start.10
  49.1 9.5 %collective-permute-done.13.refs_7_ = bf16[256,512]{1,0:T(8,128)(2,1)S(1)} collective-permute-done((bf16[256,512]{1,0:T(8,128)(2,1)S(1)}, bf16[256,512]{1,0:T(8,128)(2,1)S(1)}, u32[]{:S(2)}, u32[]{:S(2)}) %collective-permute-start.13) | collective-permute-done | bytes 262176 | tf_op jit(solution)/shard_map/ppermute | solution.py:339
  58.7 0.6 collective-permute-done.12.refs_6_
  59.6 0.6 collective-permute-start.6
  60.2 20.0 %attend.2 = (bf16[48,8192]{1,0:T(8,128)(2,1)}, bf16[48,8192]{1,0:T(8,128)(2,1)}, bf16[48,4096]{1,0:T(8,128)(2,1)}, bf16[48,4096]{1,0:T(8,128)(2,1)}, bf16[48,409...) custom-call(s32[1]{0:T(128)S(6)} %and.5.x_ref, ...), custom_call_target="tpu_custom_call" | custom-call | flops 10066329600 | bytes 8388608 | tf_op jit(solution)/shard_map/attend/pallas_call | solution.py:431
  80.3 10.6 %all-to-all-start.1 = ((bf16[4,256,512]{2,1,0:T(8,128)(2,1)}), bf16[4,256,512]{2,1,0:T(8,128)(2,1)S(1)}, u32[]{:S(2)}, u32[]{:S(2)}) async-start(bf16[4,256,512]{2,1,0:T(8,128)(2,1)} %bitcast.28), calls=%async_computation.1 | async-start | bytes 2097152 | tf_op jit(solution)/shard_map/all_to_all | solution.py:464
  90.9 0.7 copy-done.19
  91.6 20.1 %attend.3 = (bf16[48,8192]{1,0:T(8,128)(2,1)}, bf16[48,8192]{1,0:T(8,128)(2,1)}, bf16[48,4096]{1,0:T(8,128)(2,1)}, bf16[48,4096]{1,0:T(8,128)(2,1)}, bf16[48,409...) custom-call(s32[1]{0:T(128)S(6)} %and.5.x_ref, ...), custom_call_target="tpu_custom_call", output_to_operand_aliasing={{0}: (13, {}), {1}: (14, {}), {2}: (15, {}), {3}: (16, {}),... | custom-call | flops 10066329600 | bytes 8388608 | tf_op jit(solution)/shard_map/attend/pallas_call | solution.py:431
  111.7 4.4 %all-to-all-start.2 = ((bf16[4,256,512]{2,1,0:T(8,128)(2,1)}), bf16[4,256,512]{2,1,0:T(8,128)(2,1)S(1)}, u32[]{:S(2)}, u32[]{:S(2)}) async-start(bf16[4,256,512]{2,1,0:T(8,128)(2,1)} %bitcast.27), calls=%async_computation.2 | async-start | bytes 2097152 | tf_op jit(solution)/shard_map/all_to_all | solution.py:464
  116.1 3.7 %collective-permute-start.14 = (bf16[48,8192]{1,0:T(8,128)(2,1)}, bf16[48,8192]{1,0:T(8,128)(2,1)}, u32[]{:S(2)}, u32[]{:S(2)}) collective-permute-start(bf16[48,8192]{1,0:T(8,128)(2,1)} %get-tuple-element.91), channel_id=1, source_target_pairs={{0,32},{32,0},{64,96},{96,64},{128,160},{160,128},{192,224},{224,1... | collective-permute-start | bytes 2359304 | tf_op jit(solution)/shard_map/ppermute | solution.py:336
  120.1 5.1 %collective-permute-start.16 = (bf16[256,512]{1,0:T(8,128)(2,1)S(1)}, bf16[256,512]{1,0:T(8,128)(2,1)S(1)}, u32[]{:S(2)}, u32[]{:S(2)}) collective-permute-start(bf16[256,512]{1,0:T(8,128)(2,1)S(1)} %pass_on.2), channel_id=1, source_target_pairs={{4,0},{5,1},{6,2},{7,3},{8,4},{9,5},{10,6},{11,7},{12,8},{13,9},{1... | collective-permute-start | bytes 786440 | tf_op jit(solution)/shard_map/ppermute | solution.py:342
  125.2 0.4 collective-permute-start.15
  125.6 1.9 %collective-permute-start.18 = (bf16[48,4096]{1,0:T(8,128)(2,1)}, bf16[48,4096]{1,0:T(8,128)(2,1)}, u32[]{:S(2)}, u32[]{:S(2)}) collective-permute-start(bf16[48,4096]{1,0:T(8,128)(2,1)} %get-tuple-element.99), channel_id=1, source_target_pairs={{0,192},{32,224},{64,128},{96,160},{128,64},{160,96},{192,0},{224,... | collective-permute-start | bytes 1179656 | tf_op jit(solution)/shard_map/ppermute | solution.py:336
  127.5 3.5 %collective-permute-done.16.refs_1_ = bf16[256,512]{1,0:T(8,128)(2,1)S(1)} collective-permute-done((bf16[256,512]{1,0:T(8,128)(2,1)S(1)}, bf16[256,512]{1,0:T(8,128)(2,1)S(1)}, u32[]{:S(2)}, u32[]{:S(2)}) %collective-permute-start.16) | collective-permute-done | bytes 262176 | tf_op jit(solution)/shard_map/ppermute | solution.py:342
  130.9 1.1 collective-permute-start.17
  132.0 1.5 collective-permute-start.19
  133.7 2.2 %collective-permute-done.15.refs_0_ = bf16[48,4096]{1,0:T(8,128)(2,1)S(1)} collective-permute-done((bf16[48,4096]{1,0:T(8,128)(2,1)}, bf16[48,4096]{1,0:T(8,128)(2,1)S(1)}, u32[]{:S(2)}, u32[]{:S(2)}) %collective-permute-start.15) | collective-permute-done | bytes 393248 | tf_op jit(solution)/shard_map/ppermute | solution.py:336
  136.0 1.3 collective-permute-start.20
  137.2 7.9 %collective-permute-done.17.refs_1_ = bf16[48,4096]{1,0:T(8,128)(2,1)} collective-permute-done((bf16[48,4096]{1,0:T(8,128)(2,1)}, bf16[48,4096]{1,0:T(8,128)(2,1)}, u32[]{:S(2)}, u32[]{:S(2)}) %collective-permute-start.17) | collective-permute-done | bytes 393248 | tf_op jit(solution)/shard_map/ppermute | solution.py:336
  145.1 1.3 collective-permute-done.19.refs_3_
  146.4 1.7 %return_keys.1 = bf16[384,1024]{1,0:T(8,128)(2,1)} custom-call(s32[1]{0:T(128)S(6)} %and.5.x_ref, bf16[768,128]{1,0:T(8,128)(2,1)S(1)} %get-tuple-element.104.spread_ref, bf16[1024,512]{1,0:T(8,128)(2,1)S(1)} %bitcast.15, bf16[256,512]{1,0:T(8,128)(2,1)S(1)} %collective-permute-done.16.refs_1_, bf16[1024,512]{1,0:T(8,128)(2,1)S(1)} %bitcast.17, ...), custom_call_target="tpu_custom_call" | custom-call | flops 100000000 | bytes 3145728 | tf_op jit(solution)/shard_map/return_keys/pallas_call | solution.py:490
  148.1 3.5 %all-to-all-start.3 = ((bf16[8,48,1024]{2,1,0:T(8,128)(2,1)}), bf16[8,48,1024]{2,1,0:T(8,128)(2,1)S(1)}, u32[]{:S(2)}, u32[]{:S(2)}) async-start(bf16[8,48,1024]{2,1,0:T(8,128)(2,1)} %bitcast.12), calls=%async_computation.3 | async-start | bytes 1572864 | tf_op jit(solution)/shard_map/all_to_all | solution.py:498
  151.6 4.7 %unpack_rows.1 = bf16[128,8192]{1,0:T(8,128)(2,1)} custom-call(bf16[128,256]{1,0:T(8,128)(2,1)} %copy-done, bf16[48,8192]{1,0:T(8,128)(2,1)} %get-tuple-element.90.own_ref, bf16[48,8192]{1,0:T(8,128)(2,1)} %collective-permute-done.14.core_ref, bf16[48,4096]{1,0:T(8,128)(2,1)} %copy-done.14, bf16[48,4096]{1,0:T(8,128)(2,1)} %collective-permute-done.17.refs_1_, ...), custom_call_target="tpu_custom_call" | custom-call | flops 400000000 | bytes 6291456 | tf_op jit(solution)/shard_map/unpack_rows/pallas_call | solution.py:500
  156.3 7.6 %all-to-all-done.3 = bf16[8,48,1024]{2,1,0:T(8,128)(2,1)S(1)} async-done(((bf16[8,48,1024]{2,1,0:T(8,128)(2,1)}), bf16[8,48,1024]{2,1,0:T(8,128)(2,1)S(1)}, u32[]{:S(2)}, u32[]{:S(2)}) %all-to-all-start.3) | async-done | bytes 786464 | tf_op jit(solution)/shard_map/all_to_all | solution.py:498
  163.9 1.0 unpack_keys.1
  (62 shorter events, 2.0 us)
Async XLA Ops:
  0.6 13.8 %copy-start.4 = (s32[128]{0:T(128)S(1)}, s32[128]{0:T(128)}, u32[]{:S(2)}) copy-start(s32[128]{0:T(128)} %param.10) | copy-start | bytes 1540
  0.6 14.9 %collective-permute-start.1 = (bf16[128,8192]{1,0:T(8,128)(2,1)}, bf16[128,8192]{1,0:T(8,128)(2,1)S(1)}, u32[]{:S(2)}, u32[]{:S(2)}) collective-permute-start(bf16[128,8192]{1,0:T(8,128)(2,1)} %query_ref.7), channel_id=1, source_target_pairs={{0,32},{32,0},{64,96},{96,64},{128,160},{160,128},{192,224},{224,1... | collective-permute-start | bytes 6291464 | tf_op jit(solution)/shard_map/ppermute | solution.py:336
  4.0 11.6 %collective-permute-start.2 = (bf16[128,8192]{1,0:T(8,128)(2,1)}, bf16[128,8192]{1,0:T(8,128)(2,1)}, u32[]{:S(2)}, u32[]{:S(2)}) collective-permute-start(bf16[128,8192]{1,0:T(8,128)(2,1)} %grad_ref.7), channel_id=1, source_target_pairs={{0,32},{32,0},{64,96},{96,64},{128,160},{160,128},{192,224},{224,1... | collective-permute-start | bytes 6291464 | tf_op jit(solution)/shard_map/ppermute | solution.py:336
  4.8 0.7 copy-start.3
  5.5 0.9 copy-start.8
  6.4 0.9 copy-start.9
  7.3 0.7 copy-start.12
  9.9 0.6 copy-start
  10.6 17.2 %all-to-all-start = ((bf16[8,48,1152]{2,1,0:T(8,128)(2,1)}), bf16[8,48,1152]{2,1,0:T(8,128)(2,1)S(1)}, u32[]{:S(2)}, u32[]{:S(2)}) async-start(bf16[8,48,1152]{2,1,0:T(8,128)(2,1)} %bitcast.6), calls=%async_computation | async-start | bytes 1769472 | tf_op jit(solution)/shard_map/all_to_all | solution.py:357
  14.4 1.1 collective-permute-start
  15.5 0.6 copy-start.15
  15.5 1.3 copy-start.13
  27.8 18.5 %collective-permute-start.3 = (bf16[96,4096]{1,0:T(8,128)(2,1)}, bf16[96,4096]{1,0:T(8,128)(2,1)S(1)}, u32[]{:S(2)}, u32[]{:S(2)}) collective-permute-start(bf16[96,4096]{1,0:T(8,128)(2,1)} %get-tuple-element.74), channel_id=1, source_target_pairs={{0,64},{32,96},{64,0},{96,32},{128,192},{160,224},{192,128},{224,1... | collective-permute-start | bytes 2359304 | tf_op jit(solution)/shard_map/ppermute | solution.py:336
  28.1 19.5 %collective-permute-start.4 = (bf16[96,4096]{1,0:T(8,128)(2,1)}, bf16[96,4096]{1,0:T(8,128)(2,1)}, u32[]{:S(2)}, u32[]{:S(2)}) collective-permute-start(bf16[96,4096]{1,0:T(8,128)(2,1)} %get-tuple-element.75), channel_id=1, source_target_pairs={{0,192},{32,224},{64,128},{96,160},{128,64},{160,96},{192,0},{224,... | collective-permute-start | bytes 2359304 | tf_op jit(solution)/shard_map/ppermute | solution.py:336
  30.9 6.8 %copy-start.7 = (bf16[256,384]{1,0:T(8,128)(2,1)}, bf16[256,384]{1,0:T(8,128)(2,1)S(1)}, u32[]{:S(2)}) copy-start(bf16[256,384]{1,0:T(8,128)(2,1)S(1)} %get-tuple-element.63.dense_ref) | copy-start | bytes 589828
  30.9 6.8 %copy-start.10 = (bf16[144,128]{1,0:T(8,128)(2,1)}, bf16[144,128]{1,0:T(8,128)(2,1)S(1)}, u32[]{:S(2)}) copy-start(bf16[144,128]{1,0:T(8,128)(2,1)S(1)} %get-tuple-element.64.back_ref) | copy-start | bytes 110596
  30.9 6.8 %copy-start.11 = (s32[8,128]{1,0:T(8,128)}, s32[8,128]{1,0:T(8,128)S(1)}, u32[]{:S(2)}) copy-start(s32[8,128]{1,0:T(8,128)S(1)} %get-tuple-element.65.vec_ref) | copy-start | bytes 12292
  30.9 15.4 %copy-start.6 = (bf16[256,512]{1,0:T(8,128)(2,1)}, bf16[256,512]{1,0:T(8,128)(2,1)S(1)}, u32[]{:S(2)}) copy-start(bf16[256,512]{1,0:T(8,128)(2,1)S(1)} %get-tuple-element.83.refs_8_) | copy-start | bytes 786436
  30.9 28.3 %copy-start.5 = (bf16[256,512]{1,0:T(8,128)(2,1)}, bf16[256,512]{1,0:T(8,128)(2,1)S(1)}, u32[]{:S(2)}) copy-start(bf16[256,512]{1,0:T(8,128)(2,1)S(1)} %get-tuple-element.79.refs_8_) | copy-start | bytes 786436
  30.9 28.7 %collective-permute-start.8 = (bf16[256,1024]{1,0:T(8,128)(2,1)S(1)}, bf16[256,1024]{1,0:T(8,128)(2,1)}, u32[]{:S(2)}, u32[]{:S(2)}) collective-permute-start(bf16[256,1024]{1,0:T(8,128)(2,1)S(1)} %get-tuple-element.80), channel_id=1, source_target_pairs={{0,3},{1,4},{2,5},{3,6},{4,7},{5,8},{6,9},{7,10},{8,11},{9,12},{10... | collective-permute-start | bytes 1572872 | tf_op jit(solution)/shard_map/ppermute | solution.py:339
  37.7 21.5 %copy-start.17 = (bf16[96,4096]{1,0:T(8,128)(2,1)S(1)}, bf16[96,4096]{1,0:T(8,128)(2,1)}, u32[]{:S(2)}) copy-start(bf16[96,4096]{1,0:T(8,128)(2,1)} %get-tuple-element.76) | copy-start | bytes 2359300
  37.7 21.9 %copy-start.16 = (bf16[96,4096]{1,0:T(8,128)(2,1)S(1)}, bf16[96,4096]{1,0:T(8,128)(2,1)}, u32[]{:S(2)}) copy-start(bf16[96,4096]{1,0:T(8,128)(2,1)} %get-tuple-element.77) | copy-start | bytes 2359300
  42.8 15.9 %collective-permute-start.13 = (bf16[256,512]{1,0:T(8,128)(2,1)S(1)}, bf16[256,512]{1,0:T(8,128)(2,1)S(1)}, u32[]{:S(2)}, u32[]{:S(2)}) collective-permute-start(bf16[256,512]{1,0:T(8,128)(2,1)S(1)} %get-tuple-element.83.refs_8_), channel_id=1, source_target_pairs={{0,1},{1,2},{2,3},{3,4},{4,5},{5,6},{6,7},{7,8},{8,9},{9,10},{10,1... | collective-permute-start | bytes 786440 | tf_op jit(solution)/shard_map/ppermute | solution.py:339
  43.1 16.1 %collective-permute-start.12 = (bf16[256,512]{1,0:T(8,128)(2,1)S(1)}, bf16[256,512]{1,0:T(8,128)(2,1)S(1)}, u32[]{:S(2)}, u32[]{:S(2)}) collective-permute-start(bf16[256,512]{1,0:T(8,128)(2,1)S(1)} %get-tuple-element.83.refs_8_), channel_id=1, source_target_pairs={{0,2},{1,3},{2,4},{3,5},{4,6},{5,7},{6,8},{7,9},{8,10},{9,11},{10,... | collective-permute-start | bytes 786440 | tf_op jit(solution)/shard_map/ppermute | solution.py:339
  46.3 14.0 %copy-start.18 = (bf16[96,4096]{1,0:T(8,128)(2,1)}, bf16[96,4096]{1,0:T(8,128)(2,1)S(1)}, u32[]{:S(2)}) copy-start(bf16[96,4096]{1,0:T(8,128)(2,1)S(1)} %collective-permute-done.3.refs_1_) | copy-start | bytes 2359300
  46.3 12.9 %collective-permute-start.11 = (bf16[256,512]{1,0:T(8,128)(2,1)S(1)}, bf16[256,512]{1,0:T(8,128)(2,1)S(1)}, u32[]{:S(2)}, u32[]{:S(2)}) collective-permute-start(bf16[256,512]{1,0:T(8,128)(2,1)S(1)} %get-tuple-element.83.refs_8_), channel_id=1, source_target_pairs={{0,4},{1,5},{2,6},{3,7},{4,8},{5,9},{6,10},{7,11},{8,12},{9,13},{1... | collective-permute-start | bytes 786440 | tf_op jit(solution)/shard_map/ppermute | solution.py:339
  47.6 43.3 %collective-permute-start.10 = (bf16[256,512]{1,0:T(8,128)(2,1)S(1)}, bf16[256,512]{1,0:T(8,128)(2,1)S(1)}, u32[]{:S(2)}, u32[]{:S(2)}) collective-permute-start(bf16[256,512]{1,0:T(8,128)(2,1)S(1)} %get-tuple-element.79.refs_8_), channel_id=1, source_target_pairs={{0,1},{1,2},{2,3},{3,4},{4,5},{5,6},{6,7},{7,8},{8,9},{9,10},{10,1... | collective-permute-start | bytes 786440 | tf_op jit(solution)/shard_map/ppermute | solution.py:339
  58.7 1.6 copy-start.20
  58.7 32.3 %collective-permute-start.9 = (bf16[256,512]{1,0:T(8,128)(2,1)S(1)}, bf16[256,512]{1,0:T(8,128)(2,1)}, u32[]{:S(2)}, u32[]{:S(2)}) collective-permute-start(bf16[256,512]{1,0:T(8,128)(2,1)S(1)} %get-tuple-element.79.refs_8_), channel_id=1, source_target_pairs={{0,2},{1,3},{2,4},{3,5},{4,6},{5,7},{6,8},{7,9},{8,10},{9,11},{10,... | collective-permute-start | bytes 786440 | tf_op jit(solution)/shard_map/ppermute | solution.py:339
  59.2 1.0 copy-start.21
  59.2 31.7 %collective-permute-start.7 = (bf16[256,512]{1,0:T(8,128)(2,1)S(1)}, bf16[256,512]{1,0:T(8,128)(2,1)}, u32[]{:S(2)}, u32[]{:S(2)}) collective-permute-start(bf16[256,512]{1,0:T(8,128)(2,1)S(1)} %get-tuple-element.79.refs_8_), channel_id=1, source_target_pairs={{0,4},{1,5},{2,6},{3,7},{4,8},{5,9},{6,10},{7,11},{8,12},{9,13},{1... | collective-permute-start | bytes 786440 | tf_op jit(solution)/shard_map/ppermute | solution.py:339
  59.2 1.0 copy-start.22
  59.3 31.7 %collective-permute-start.5 = (bf16[96,4096]{1,0:T(8,128)(2,1)S(1)}, bf16[96,4096]{1,0:T(8,128)(2,1)}, u32[]{:S(2)}, u32[]{:S(2)}) collective-permute-start(bf16[96,4096]{1,0:T(8,128)(2,1)S(1)} %copy-done.17), channel_id=1, source_target_pairs={{0,64},{32,96},{64,0},{96,32},{128,192},{160,224},{192,128},{224,1... | collective-permute-start | bytes 2359304 | tf_op jit(solution)/shard_map/ppermute | solution.py:336
  59.6 31.3 %collective-permute-start.6 = (bf16[96,4096]{1,0:T(8,128)(2,1)S(1)}, bf16[96,4096]{1,0:T(8,128)(2,1)}, u32[]{:S(2)}, u32[]{:S(2)}) collective-permute-start(bf16[96,4096]{1,0:T(8,128)(2,1)S(1)} %copy-done.16), channel_id=1, source_target_pairs={{0,192},{32,224},{64,128},{96,160},{128,64},{160,96},{192,0},{224,... | collective-permute-start | bytes 2359304 | tf_op jit(solution)/shard_map/ppermute | solution.py:336
  80.3 31.4 %all-to-all-start.1 = ((bf16[4,256,512]{2,1,0:T(8,128)(2,1)}), bf16[4,256,512]{2,1,0:T(8,128)(2,1)S(1)}, u32[]{:S(2)}, u32[]{:S(2)}) async-start(bf16[4,256,512]{2,1,0:T(8,128)(2,1)} %bitcast.28), calls=%async_computation.1 | async-start | bytes 2097152 | tf_op jit(solution)/shard_map/all_to_all | solution.py:464
  90.9 0.7 copy-start.19
  111.7 8.1 %copy-start.1 = (bf16[256,512]{1,0:T(8,128)(2,1)S(1)}, bf16[256,512]{1,0:T(8,128)(2,1)}, u32[]{:S(2)}) copy-start(bf16[256,512]{1,0:T(8,128)(2,1)} %get-tuple-element.97.far_ref) | copy-start | bytes 786436
  111.7 21.8 %copy-start.2 = (bf16[256,512]{1,0:T(8,128)(2,1)S(1)}, bf16[256,512]{1,0:T(8,128)(2,1)}, u32[]{:S(2)}) copy-start(bf16[256,512]{1,0:T(8,128)(2,1)} %get-tuple-element.95.far_ref) | copy-start | bytes 786436
  111.7 21.7 %all-to-all-start.2 = ((bf16[4,256,512]{2,1,0:T(8,128)(2,1)}), bf16[4,256,512]{2,1,0:T(8,128)(2,1)S(1)}, u32[]{:S(2)}, u32[]{:S(2)}) async-start(bf16[4,256,512]{2,1,0:T(8,128)(2,1)} %bitcast.27), calls=%async_computation.2 | async-start | bytes 2097152 | tf_op jit(solution)/shard_map/all_to_all | solution.py:464
  116.1 30.3 %collective-permute-start.14 = (bf16[48,8192]{1,0:T(8,128)(2,1)}, bf16[48,8192]{1,0:T(8,128)(2,1)}, u32[]{:S(2)}, u32[]{:S(2)}) collective-permute-start(bf16[48,8192]{1,0:T(8,128)(2,1)} %get-tuple-element.91), channel_id=1, source_target_pairs={{0,32},{32,0},{64,96},{96,64},{128,160},{160,128},{192,224},{224,1... | collective-permute-start | bytes 2359304 | tf_op jit(solution)/shard_map/ppermute | solution.py:336
  120.1 10.9 %collective-permute-start.16 = (bf16[256,512]{1,0:T(8,128)(2,1)S(1)}, bf16[256,512]{1,0:T(8,128)(2,1)S(1)}, u32[]{:S(2)}, u32[]{:S(2)}) collective-permute-start(bf16[256,512]{1,0:T(8,128)(2,1)S(1)} %pass_on.2), channel_id=1, source_target_pairs={{4,0},{5,1},{6,2},{7,3},{8,4},{9,5},{10,6},{11,7},{12,8},{13,9},{1... | collective-permute-start | bytes 786440 | tf_op jit(solution)/shard_map/ppermute | solution.py:342
  125.2 10.7 %collective-permute-start.15 = (bf16[48,4096]{1,0:T(8,128)(2,1)}, bf16[48,4096]{1,0:T(8,128)(2,1)S(1)}, u32[]{:S(2)}, u32[]{:S(2)}) collective-permute-start(bf16[48,4096]{1,0:T(8,128)(2,1)} %get-tuple-element.92), channel_id=1, source_target_pairs={{0,64},{32,96},{64,0},{96,32},{128,192},{160,224},{192,128},{224,1... | collective-permute-start | bytes 1179656 | tf_op jit(solution)/shard_map/ppermute | solution.py:336
  125.6 11.6 %collective-permute-start.18 = (bf16[48,4096]{1,0:T(8,128)(2,1)}, bf16[48,4096]{1,0:T(8,128)(2,1)}, u32[]{:S(2)}, u32[]{:S(2)}) collective-permute-start(bf16[48,4096]{1,0:T(8,128)(2,1)} %get-tuple-element.99), channel_id=1, source_target_pairs={{0,192},{32,224},{64,128},{96,160},{128,64},{160,96},{192,0},{224,... | collective-permute-start | bytes 1179656 | tf_op jit(solution)/shard_map/ppermute | solution.py:336
  130.9 14.2 %collective-permute-start.17 = (bf16[48,4096]{1,0:T(8,128)(2,1)}, bf16[48,4096]{1,0:T(8,128)(2,1)}, u32[]{:S(2)}, u32[]{:S(2)}) collective-permute-start(bf16[48,4096]{1,0:T(8,128)(2,1)} %get-tuple-element.98), channel_id=1, source_target_pairs={{0,96},{32,64},{64,32},{96,0},{128,224},{160,192},{192,160},{224,1... | collective-permute-start | bytes 1179656 | tf_op jit(solution)/shard_map/ppermute | solution.py:336
  132.0 14.4 %collective-permute-start.19 = (bf16[48,4096]{1,0:T(8,128)(2,1)}, bf16[48,4096]{1,0:T(8,128)(2,1)}, u32[]{:S(2)}, u32[]{:S(2)}) collective-permute-start(bf16[48,4096]{1,0:T(8,128)(2,1)} %get-tuple-element.101), channel_id=1, source_target_pairs={{0,224},{32,192},{64,160},{96,128},{128,96},{160,64},{192,32},{224... | collective-permute-start | bytes 1179656 | tf_op jit(solution)/shard_map/ppermute | solution.py:336
  136.0 12.1 %copy-start.14 = (bf16[48,4096]{1,0:T(8,128)(2,1)}, bf16[48,4096]{1,0:T(8,128)(2,1)S(1)}, u32[]{:S(2)}) copy-start(bf16[48,4096]{1,0:T(8,128)(2,1)S(1)} %collective-permute-done.15.refs_0_) | copy-start | bytes 1179652
  136.0 10.4 %collective-permute-start.20 = (bf16[256,512]{1,0:T(8,128)(2,1)S(1)}, bf16[256,512]{1,0:T(8,128)(2,1)S(1)}, u32[]{:S(2)}, u32[]{:S(2)}) collective-permute-start(bf16[256,512]{1,0:T(8,128)(2,1)S(1)} %pass_on.3), channel_id=1, source_target_pairs={{4,0},{5,1},{6,2},{7,3},{8,4},{9,5},{10,6},{11,7},{12,8},{13,9},{1... | collective-permute-start | bytes 786440 | tf_op jit(solution)/shard_map/ppermute | solution.py:342
  148.1 15.8 %all-to-all-start.3 = ((bf16[8,48,1024]{2,1,0:T(8,128)(2,1)}), bf16[8,48,1024]{2,1,0:T(8,128)(2,1)S(1)}, u32[]{:S(2)}, u32[]{:S(2)}) async-start(bf16[8,48,1024]{2,1,0:T(8,128)(2,1)} %bitcast.12), calls=%async_computation.3 | async-start | bytes 1572864 | tf_op jit(solution)/shard_map/all_to_all | solution.py:498
